TPU v7x, 1024 devices: a whole 8x8x8 slice. The times are simulated.
1024 devices in a mesh: fsdp: 32 (over z, x_lo), dp: 32 (over y, x_hi, core).
Axes of the slice: x: 8 (x_hi: 2, x_lo: 4; x = x_hi * 4 + x_lo), y: 8, z: 8, core: 2. Of those that a mesh axis runs over, the one named last changes fastest.
Arguments:
- tokens: bfloat16 [32, 6144, 4096], P('dp', 'fsdp'), may hold values from -9 to 9
- segment_ids: int32 [32, 6144], P('dp'), may hold values from 0 to 95, never falling along the last dimension, each value on 1 to 192 neighbouring positions
- w_query: bfloat16 [4096, 128], P('fsdp'), may hold values from -0.2 to 0.2
- w_key: bfloat16 [4096, 128], P('fsdp'), may hold values from -0.2 to 0.2
- w_value: bfloat16 [4096, 128], P('fsdp'), may hold values from -0.09375 to 0.09375
- grad_out: bfloat16 [32, 6144, 128], P('dp', 'fsdp'), may hold values from -6 to 6
Outputs:
- attn: bfloat16 [32, 6144, 128], P('dp', 'fsdp')
- grad_tokens: bfloat16 [32, 6144, 4096], P('dp', 'fsdp')
- grad_query: float32 [4096, 128], P(('fsdp', 'dp'))
- grad_key: float32 [4096, 128], P(('fsdp', 'dp'))
- grad_value: float32 [4096, 128], P(('fsdp', 'dp'))
Inputs may be any that keep to these rules, and one draw needn't show every extreme that they name: `segment_ids`: ids never fall along a sequence; every document has 1 to 192 tokens and some document has exactly 192.
All inputs are finite; a program needn't handle non-finite values.
Results may differ from a plain program's by a relative error of at most 0.03.
Values may be sent and summed in bfloat16 or wider, within the bound.
No kernel may reach another device: no remote copies, remote signals or barrier semaphores. Data moves between devices by JAX's collectives and lax.ppermute only.
A program may use at most 32 MiB of HBM per device.

v0:
```python
import math

import jax
import jax.numpy as jnp
from jax import lax
from jax.sharding import PartitionSpec as P


def shifted(block, axis, distance):
    devices = range(lax.axis_size(axis))
    route = [(i - distance, i) for i in devices if i - distance in devices]
    return lax.ppermute(block, axis, route)


def local(tokens, segment_ids, w_query, w_key, w_value, grad_out):
    tok_rows = tokens[0]
    tok_count = tok_rows.shape[0]
    heads = w_query.shape[1]
    group_count = lax.axis_size("dp")
    loop_count = lax.axis_size("fsdp")
    local_weight = jnp.concatenate([w_query, w_key, w_value], axis=1)
    full_weight = lax.all_gather(local_weight, "fsdp", axis=0, tiled=True)
    projected = jnp.dot(tok_rows, full_weight, preferred_element_type=jnp.float32)
    qkv_rounded = projected.astype(jnp.bfloat16)
    query_rows = qkv_rounded[:, :heads]
    own_keys = qkv_rounded[:, heads : 2 * heads]
    own_values = qkv_rounded[:, 2 * heads :]
    earlier = shifted(jnp.stack([own_keys, own_values]), "fsdp", 1)
    packed_key_rows = jnp.concatenate([earlier[0], own_keys], axis=0)
    packed_value_rows = jnp.concatenate([earlier[1], own_values], axis=0)
    device = lax.axis_index("fsdp")
    first_row = device * tok_count
    id_line = segment_ids[0]
    own_ids = lax.dynamic_slice_in_dim(id_line, first_row, tok_count)
    prior_ids = lax.dynamic_slice_in_dim(id_line, jnp.maximum(first_row - tok_count, 0), tok_count)
    key_ids = jnp.concatenate([prior_ids, own_ids])
    query_pos = first_row + jnp.arange(tok_count, dtype=jnp.int32)
    key_pos = first_row - tok_count + jnp.arange(2 * tok_count, dtype=jnp.int32)
    allowed = (
        (key_pos[None, :] <= query_pos[:, None])
        & (key_pos[None, :] >= 0)
        & (key_ids[None, :] == own_ids[:, None])
    )
    softmax_scale = 1.0 / math.sqrt(heads)
    logit_scores = (
        lax.dot_general(
            query_rows,
            packed_key_rows,
            (((1,), (1,)), ((), ())),
            preferred_element_type=jnp.float32,
        )
        * softmax_scale
    )
    logit_scores = jnp.where(allowed, logit_scores, -1e30)
    peak = jnp.max(logit_scores, axis=-1, keepdims=True)
    weights_exp = jnp.where(allowed, jnp.exp(logit_scores - peak), 0.0)
    prob = weights_exp / jnp.sum(weights_exp, axis=-1, keepdims=True)
    probability_batch = prob.astype(jnp.bfloat16)
    attn = jnp.dot(probability_batch, packed_value_rows, preferred_element_type=jnp.float32).astype(
        jnp.bfloat16
    )
    upstream = grad_out[0]
    probability_gradient = lax.dot_general(
        upstream, packed_value_rows, (((1,), (1,)), ((), ())), preferred_element_type=jnp.float32
    )
    delta = jnp.sum(prob * probability_gradient, axis=-1, keepdims=True)
    score_gradient = (prob * (probability_gradient - delta) * softmax_scale).astype(jnp.bfloat16)
    query_gradient = jnp.dot(
        score_gradient, packed_key_rows, preferred_element_type=jnp.float32
    ).astype(jnp.bfloat16)
    key_gradient_parts = lax.dot_general(
        score_gradient, query_rows, (((0,), (0,)), ((), ())), preferred_element_type=jnp.float32
    )
    value_gradient_parts = lax.dot_general(
        probability_batch, upstream, (((0,), (0,)), ((), ())), preferred_element_type=jnp.float32
    )
    returned = shifted(
        jnp.stack([key_gradient_parts[:tok_count], value_gradient_parts[:tok_count]]), "fsdp", -1
    )
    grad_k = (key_gradient_parts[tok_count:] + returned[0]).astype(jnp.bfloat16)
    grad_v = (value_gradient_parts[tok_count:] + returned[1]).astype(jnp.bfloat16)
    grad_proj = jnp.concatenate([query_gradient, grad_k, grad_v], axis=1)
    grad_input = lax.dot_general(
        grad_proj, full_weight, (((1,), (1,)), ((), ())), preferred_element_type=jnp.float32
    ).astype(jnp.bfloat16)
    term = lax.dot_general(
        tok_rows, grad_proj, (((0,), (0,)), ((), ())), preferred_element_type=jnp.float32
    )
    loop_total = lax.psum_scatter(
        term.astype(jnp.bfloat16), "fsdp", scatter_dimension=0, tiled=True
    ).astype(jnp.float32)
    replica_total = lax.psum_scatter(loop_total, "dp", scatter_dimension=0, tiled=True)
    grads = replica_total * (1.0 / math.sqrt(group_count * loop_count * tok_count))
    return (
        attn[None],
        grad_input[None],
        grads[:, :heads],
        grads[:, heads : 2 * heads],
        grads[:, 2 * heads :],
    )


def solution(mesh):
    in_specs = (
        P("dp", "fsdp", None),
        P("dp", None),
        P("fsdp", None),
        P("fsdp", None),
        P("fsdp", None),
        P("dp", "fsdp", None),
    )
    out_specs = (
        P("dp", "fsdp", None),
        P("dp", "fsdp", None),
        P(("fsdp", "dp"), None),
        P(("fsdp", "dp"), None),
        P(("fsdp", "dp"), None),
    )
    return jax.shard_map(local, mesh=mesh, in_specs=in_specs, out_specs=out_specs, check_vma=False)
```

profile of v0, /device:TPU:1, one launch (start us, length us, event | category | flops | bytes accessed | tf_op | source)
XLA Modules:
  0.0 566.5 jit_solution(17204622281299537027)
XLA Ops:
  7.2 0.0 all-gather.2.cloned.1.call-start
  7.2 1.6 pad_maximum_fusion.2
  8.8 0.0 all-gather.2.cloned.1.call-update
  8.8 0.0 reduce-scatter.5.cloned.1.call-start
  8.9 0.8 constant_dynamic-slice_fusion.1
  9.7 0.1 pad_add_fusion
  9.8 161.8 %all-gather.2.cloned.1.call-done = bf16[4096,384]{1,0:T(8,128)(2,1)} async-done(((bf16[128,384]{1,0:T(8,128)(2,1)}), bf16[4096,384]{1,0:T(8,128)(2,1)}) %all-gather.2.cloned.1.call-update) | async-done | bytes 3145744 | tf_op jit(solution)/shard_map/all_gather | solution.py:22
  171.6 2.9 fusion.9
  174.5 1.4 collective-permute-start
  175.9 1.6 collective-permute-done
  177.6 0.3 fusion.36
  177.9 0.3 fusion.14
  178.2 0.3 multiply_reduce_fusion
  178.5 0.3 fusion.19
  178.8 0.1 multiply_convert_fusion
  178.9 0.2 fusion.24
  179.2 1.3 collective-permute-start.1
  180.5 0.2 convolution_convert_fusion.2
  180.7 6.4 %collective-permute-done.1 = f32[2,192,128]{2,1,0:T(8,128)S(1)} collective-permute-done((f32[2,192,128]{2,1,0:T(8,128)S(1)}, f32[2,192,128]{2,1,0:T(8,128)S(1)}, u32[]{:S(2)}, u32[]{:S(2)}) %collective-permute-start.1) | collective-permute-done | bytes 196640 | tf_op jit(solution)/shard_map/ppermute | solution.py:12
  187.1 2.7 fusion
  189.8 4.6 copy.17
  194.4 0.0 reduce-scatter.5.cloned.1.call-update
  194.4 1.3 dynamic-slice.2
  196.4 0.8 fusion.12
  197.2 4.3 fusion.1
  201.5 171.0 %reduce-scatter.5.cloned.1.call-done = bf16[128,384]{1,0:T(8,128)(2,1)} async-done(((bf16[4096,384]{1,0:T(8,128)(2,1)}), bf16[128,384]{1,0:T(8,128)(2,1)}) %reduce-scatter.5.cloned.1.call-update) | async-done | bytes 98320
  372.5 1.0 copy.18
  373.5 184.0 %all-reduce.2 = f32[128,384]{0,1:T(8,128)S(1)} all-reduce(bf16[128,384]{0,1:T(8,128)(2,1)S(1)} %copy.18), channel_id=3, replica_groups=mesh['fsdp'=32,'dp'=32] {'dp'}, use_global_device_ids=true, to_apply=%region_4.5.clone | all-reduce | flops 49152 | bytes 294912
  557.5 0.1 dynamic-slice_multiply_fusion
  557.7 0.7 copy.14
  558.3 0.7 copy.15
  559.0 0.7 copy.16
  (14 shorter events, 0.1 us)
Async XLA Ops:
  7.2 164.4 %copy-start = (bf16[1,192,4096]{2,1,0:T(8,128)(2,1)S(1)}, bf16[1,192,4096]{2,1,0:T(8,128)(2,1)}, u32[]{:S(2)}) copy-start(bf16[1,192,4096]{2,1,0:T(8,128)(2,1)} %param.6) | copy-start | bytes 4718596
  7.2 164.4 %all-gather.2.cloned.1.call-start = ((), (), s32[]{:S(2)}) async-start(), calls=%async_computation.1 | async-start | bytes 3244032 | tf_op jit(solution)/shard_map/all_gather | solution.py:22
  8.8 363.7 %reduce-scatter.5.cloned.1.call-start = ((), (), s32[]{:S(2)}) async-start(), calls=%async_computation.2 | async-start | bytes 3244032
  9.8 168.4 %copy-start.1 = (bf16[1,192,128]{2,1,0:T(8,128)(2,1)S(1)}, bf16[1,192,128]{2,1,0:T(8,128)(2,1)}, u32[]{:S(2)}) copy-start(bf16[1,192,128]{2,1,0:T(8,128)(2,1)} %param.11) | copy-start | bytes 147460
  174.5 3.1 collective-permute-start
  179.2 7.8 %collective-permute-start.1 = (f32[2,192,128]{2,1,0:T(8,128)S(1)}, f32[2,192,128]{2,1,0:T(8,128)S(1)}, u32[]{:S(2)}, u32[]{:S(2)}) collective-permute-start(f32[2,192,128]{2,1,0:T(8,128)S(1)} %pad_maximum_fusion), channel_id=1, source_target_pairs={{32,0},{64,32},{96,64},{128,96},{160,128},{192,160},{224,192},{256... | collective-permute-start | bytes 589832 | tf_op jit(solution)/shard_map/ppermute | solution.py:12
Sparse Core Ops, SparseCore 0:
  11.3 160.2 all-gather.1
  194.6 177.8 reduce-scatter.4
where the time goes:
time: 573 us; the launch traced here: 566 us
  waiting for transfers between devices  341 us (60%)
  blocking collectives  184 us (32%)
  between operations  14.9 us (3%)
  matrix products  12 us (2%)
  local copies, waits for them, and re-layouts  9.8 us (2%)
    unnamed x1, blocking collectives  184 us
    unnamed x3, waiting for transfers between devices  171 us
    all_gather x1, waiting for transfers between devices, local(): full_weight = lax.all_gather(local_weight, 'fsdp', axis=0, tiled=True)  162 us
  transfers between devices with their start and end apart: 4, of which 4 were waited for; matrix products, arithmetic and copies ran while one was open for 1% of the time, Pallas kernels for 0%

commit v1 on v0

v1 whole, which is shorter than its diff:
```python
import functools
import math

import jax
import jax.numpy as jnp
from jax import lax
from jax.experimental import pallas as pl
from jax.experimental.pallas import tpu as pltpu
from jax.sharding import Mesh
from jax.sharding import PartitionSpec as P

FSDP = ("zh", "zl", "xlh", "xll")
DP = ("yh", "yl", "xh", "c")
SIZES = (4, 2, 2, 2, 4, 2, 2, 2)
CUBE = ("zl", "xll", "yl")
SWAP = [(0, 1), (1, 0)]
VMEM = 48 * 1024 * 1024


def fsdp_index(zh, zl, xlh, xll):
    return ((zh * 2 + zl) * 2 + xlh) * 2 + xll


def shifted(block, distance):
    route = [(i - distance, i) for i in range(32) if 0 <= i - distance < 32]
    return lax.ppermute(block, FSDP, route)


def project_kernel(core_ref, tok_ref, mine_ref, other_ref, weight_ref, qkv_ref):
    core = core_ref[0]
    for zl in range(2):
        for xll in range(2):
            for yl in range(2):
                for zh in range(4):
                    for xlh in range(2):
                        row = fsdp_index(zh, zl, xlh, xll) * 128 + yl * 32
                        at = (zl * 2 + xll) * 2 + yl, zh * 2 + xlh
                        here = pl.multiple_of(row + core * 64, 32)
                        there = pl.multiple_of(row + (1 - core) * 64, 32)
                        weight_ref[pl.ds(here, 32), :] = mine_ref[at]
                        weight_ref[pl.ds(there, 32), :] = other_ref[at]
    qkv_ref[...] = jnp.dot(
        tok_ref[...], weight_ref[...], preferred_element_type=jnp.float32
    ).astype(jnp.bfloat16)


def term_kernel(core_ref, tok_ref, grad_ref, mine_ref, other_ref):
    first = core_ref[0] == 0
    grad = grad_ref[...]
    columns = grad.shape[1]
    low = lax.broadcasted_iota(jnp.int32, (8, 8, columns), 1) < 4
    for zh in range(4):
        for zl in range(2):
            for xlh in range(2):
                for xll in range(2):
                    f = fsdp_index(zh, zl, xlh, xll)
                    term = lax.dot_general(
                        tok_ref[:, f * 128 : (f + 1) * 128],
                        grad,
                        (((0,), (0,)), ((), ())),
                        preferred_element_type=jnp.float32,
                    )
                    by_hi = term.reshape(8, 2, 8, columns)
                    even, odd = by_hi[:, 0], by_hi[:, 1]
                    zero = jnp.where(low, even, pltpu.roll(odd, 4, 1))
                    one = jnp.where(low, pltpu.roll(even, 4, 1), odd)
                    mine = jnp.where(first, zero, one).reshape(4, 2, 8, columns)
                    other = jnp.where(first, one, zero).reshape(4, 2, 8, columns)
                    for yl in range(2):
                        at = (zl * 2 + xll) * 2 + yl, zh * 2 + xlh
                        mine_ref[at] = mine[:, yl].reshape(32, columns).astype(jnp.bfloat16)
                        other_ref[at] = other[:, yl].reshape(32, columns).astype(jnp.bfloat16)


def whole(memory=pltpu.VMEM):
    return pl.BlockSpec(memory_space=memory)


def call(kernel, outs, flops, moved, *args):
    return pl.pallas_call(
        kernel,
        out_shape=[jax.ShapeDtypeStruct(shape, jnp.bfloat16) for shape in outs],
        in_specs=[whole(pltpu.SMEM)] + [whole() for _ in args[1:]],
        out_specs=[whole() for _ in outs],
        compiler_params=pltpu.CompilerParams(vmem_limit_bytes=VMEM),
        cost_estimate=pl.CostEstimate(flops=flops, bytes_accessed=moved, transcendentals=0),
    )(*args)


def local(tokens, segment_ids, w_query, w_key, w_value, grad_out):
    tok_rows = tokens[0]
    tok_count, depth = tok_rows.shape
    heads = w_query.shape[1]
    core = lax.axis_index("c")
    core_arg = core.reshape(1).astype(jnp.int32)
    flops, moved = 2 * tok_count * depth * 3 * heads, 3 * 2 * tok_count * depth

    local_weight = jnp.concatenate([w_query, w_key, w_value], axis=1)
    start = core * 64 + lax.axis_index("yl") * 32
    quarter = lax.dynamic_slice_in_dim(local_weight, start, 32, axis=0)
    far = lax.all_to_all(jnp.broadcast_to(quarter, (8,) + quarter.shape), ("zh", "xlh"), 0, 0)
    half = lax.all_to_all(jnp.broadcast_to(far, (8,) + far.shape), CUBE, 0, 0)
    other_half = lax.ppermute(half, "c", SWAP)
    full_weight, qkv_rounded = call(
        project_kernel,
        [(depth, 3 * heads), (tok_count, 3 * heads)],
        flops,
        moved,
        core_arg,
        tok_rows,
        half,
        other_half,
    )

    query_rows = qkv_rounded[:, :heads]
    own_keys = qkv_rounded[:, heads : 2 * heads]
    own_values = qkv_rounded[:, 2 * heads :]
    earlier = shifted(qkv_rounded[:, heads:], 1)
    packed_key_rows = jnp.concatenate([earlier[:, :heads], own_keys], axis=0)
    packed_value_rows = jnp.concatenate([earlier[:, heads:], own_values], axis=0)
    device = lax.axis_index(FSDP)
    first_row = device * tok_count
    id_line = segment_ids[0]
    own_ids = lax.dynamic_slice_in_dim(id_line, first_row, tok_count)
    prior_ids = lax.dynamic_slice_in_dim(id_line, jnp.maximum(first_row - tok_count, 0), tok_count)
    key_ids = jnp.concatenate([prior_ids, own_ids])
    query_pos = first_row + jnp.arange(tok_count, dtype=jnp.int32)
    key_pos = first_row - tok_count + jnp.arange(2 * tok_count, dtype=jnp.int32)
    allowed = (
        (key_pos[None, :] <= query_pos[:, None])
        & (key_pos[None, :] >= 0)
        & (key_ids[None, :] == own_ids[:, None])
    )
    softmax_scale = 1.0 / math.sqrt(heads)
    logit_scores = (
        lax.dot_general(
            query_rows,
            packed_key_rows,
            (((1,), (1,)), ((), ())),
            preferred_element_type=jnp.float32,
        )
        * softmax_scale
    )
    logit_scores = jnp.where(allowed, logit_scores, -1e30)
    peak = jnp.max(logit_scores, axis=-1, keepdims=True)
    weights_exp = jnp.where(allowed, jnp.exp(logit_scores - peak), 0.0)
    prob = weights_exp / jnp.sum(weights_exp, axis=-1, keepdims=True)
    probability_batch = prob.astype(jnp.bfloat16)
    attn = jnp.dot(probability_batch, packed_value_rows, preferred_element_type=jnp.float32).astype(
        jnp.bfloat16
    )
    upstream = grad_out[0]
    probability_gradient = lax.dot_general(
        upstream, packed_value_rows, (((1,), (1,)), ((), ())), preferred_element_type=jnp.float32
    )
    delta = jnp.sum(prob * probability_gradient, axis=-1, keepdims=True)
    score_gradient = (prob * (probability_gradient - delta) * softmax_scale).astype(jnp.bfloat16)
    query_gradient = jnp.dot(
        score_gradient, packed_key_rows, preferred_element_type=jnp.float32
    ).astype(jnp.bfloat16)
    key_gradient_parts = lax.dot_general(
        score_gradient, query_rows, (((0,), (0,)), ((), ())), preferred_element_type=jnp.float32
    )
    value_gradient_parts = lax.dot_general(
        probability_batch, upstream, (((0,), (0,)), ((), ())), preferred_element_type=jnp.float32
    )
    returned = shifted(
        jnp.stack([key_gradient_parts[:tok_count], value_gradient_parts[:tok_count]]), -1
    )
    grad_k = (key_gradient_parts[tok_count:] + returned[0]).astype(jnp.bfloat16)
    grad_v = (value_gradient_parts[tok_count:] + returned[1]).astype(jnp.bfloat16)
    grad_proj = jnp.concatenate([query_gradient, grad_k, grad_v], axis=1)

    parts = (8, 8, 32, 3 * heads)
    mine, other = call(
        term_kernel, [parts, parts], flops, moved, core_arg, tok_rows, grad_proj
    )
    swapped = lax.ppermute(other, "c", SWAP)
    grad_input = lax.dot_general(
        grad_proj, full_weight, (((1,), (1,)), ((), ())), preferred_element_type=jnp.float32
    ).astype(jnp.bfloat16)
    chip = (mine.astype(jnp.float32) + swapped.astype(jnp.float32)).astype(jnp.bfloat16)
    cube = jnp.sum(lax.all_to_all(chip, CUBE, 0, 0).astype(jnp.float32), axis=0)
    rows = cube.astype(jnp.bfloat16).reshape(64, 4, 3 * heads)
    rows = lax.all_to_all(rows, ("zh", "xlh", "yh", "xh"), 0, 0)
    count = math.prod(lax.axis_size(name) for name in FSDP + DP) * tok_count
    grads = jnp.sum(rows.astype(jnp.float32), axis=0) * (1.0 / math.sqrt(count))
    return (
        attn[None],
        grad_input[None],
        grads[:, :heads],
        grads[:, heads : 2 * heads],
        grads[:, 2 * heads :],
    )


def solution(mesh):
    fine = Mesh(mesh.devices.reshape(SIZES), FSDP + DP)
    rows = P(DP, FSDP, None)
    weight = P(FSDP, None)
    gradient = P(FSDP + DP, None)
    return jax.shard_map(
        local,
        mesh=fine,
        in_specs=(rows, P(DP, None), weight, weight, weight, rows),
        out_specs=(rows, rows, gradient, gradient, gradient),
        check_vma=False,
    )
```

time: 573 us -> 147 us (0.26); the launches traced: 566 us -> 146 us
  waiting for transfers between devices: 341 us -> 25.7 us
  blocking collectives: 184 us -> 75.5 us
  starting transfers between devices: 2.81 us -> 28 us
  between operations: 14.9 us -> 0.92 us
  local copies, waits for them, and re-layouts: 9.8 us -> 2.44 us
    unnamed x1 -> x0, blocking collectives: 184 us -> none
    unnamed x3 -> x0, waiting for transfers between devices: 171 us -> none
    all_gather x1 -> x0, waiting for transfers between devices: 162 us -> none  [local(): full_weight = lax.all_gather(local_weight, 'fsdp', axis=0, tiled=True)]
    all_to_all x0 -> x3, blocking collectives: none -> 75.5 us  [the longest x1 27 us: local(): lax.all_to_all(jnp.broadcast_to(quarter, (8,) + quarter.shape), ('zh', 'x...]
    all_to_all x0 -> x1, starting transfers between devices: none -> 15.2 us  [local(): rows = lax.all_to_all(rows, ('zh', 'xlh', 'yh', 'xh'), 0, 0)]
    all_to_all x0 -> x1, waiting for transfers between devices: none -> 11.3 us  [local(): rows = lax.all_to_all(rows, ('zh', 'xlh', 'yh', 'xh'), 0, 0)]
    ppermute x2 -> x4, starting transfers between devices: 2.73 us -> 12.8 us  [the longest x1 5.95 us: local(): other_half = lax.ppermute(half, 'c', SWAP)]
    unnamed x10 -> x20, local copies, waits for them, and re-layouts: 8.89 us -> 0.05 us
  transfers between devices with their start and end apart: 4 -> 5, of which waited for: 4 -> 5; matrix products, arithmetic and copies ran while one was open for 1% -> 4% of each run, Pallas kernels for 0% -> 0%
where the time goes in v1:
time: 147 us; the launch traced here: 146 us
  blocking collectives  75.5 us (51%)
  starting transfers between devices  28 us (19%)
  waiting for transfers between devices  25.7 us (17%)
  matrix products  6.42 us (4%)
  Pallas kernels  5.51 us (4%)
  local copies, waits for them, and re-layouts  2.44 us (2%)
  other arithmetic  2 us (1%)
    all_to_all x1, blocking collectives, local(): lax.all_to_all(jnp.broadcast_to(quarter, (8,) + quarter.shape), ('zh', 'x...  27 us
    all_to_all x1, blocking collectives, local(): cube = jnp.sum(lax.all_to_all(chip, CUBE, 0, 0).astype(jnp.float32), axis=0)  25 us
    all_to_all x1, blocking collectives, local(): half = lax.all_to_all(jnp.broadcast_to(far, (8,) + far.shape), CUBE, 0, 0)  23.5 us
    all_to_all x1, starting transfers between devices, local(): rows = lax.all_to_all(rows, ('zh', 'xlh', 'yh', 'xh'), 0, 0)  15.2 us
    all_to_all x1, waiting for transfers between devices, local(): rows = lax.all_to_all(rows, ('zh', 'xlh', 'yh', 'xh'), 0, 0)  11.3 us
    ppermute x2, waiting for transfers between devices, shifted(): return lax.ppermute(block, FSDP, route)  9.19 us
    ppermute x1, starting transfers between devices, local(): other_half = lax.ppermute(half, 'c', SWAP)  5.95 us
    pallas_call x2, Pallas kernels, call(): pl.pallas_call(kernel, out_shape=[jax.ShapeDtypeStruct(shape, jnp.bfloat1...  5.51 us
  transfers between devices with their start and end apart: 5, of which 5 were waited for; matrix products, arithmetic and copies ran while one was open for 4% of the time, Pallas kernels for 0%

profile of v1, /device:TPU:1, one launch (start us, length us, event | category | flops | bytes accessed | tf_op | source)
XLA Modules:
  0.0 146.5 jit_solution(17798098329526785689)
XLA Ops:
  0.7 0.7 fusion.18
  1.4 27.0 %all_to_all.20 = bf16[8,32,384]{2,1,0:T(8,128)(2,1)S(1)} all-to-all(bf16[8,32,384]{2,1,0:T(8,128)(2,1)S(1)} %broadcast_in_dim.27), channel_id=1, replica_groups=mesh['zh'=4,'zl'=2,'xlh'=2,'xll'=2,'yh'=4,'yl'=2,'xh'=2,'c'=2] {'zh','xlh'}, dimensions={0} | all-to-all | bytes 393216 | tf_op jit(solution)/shard_map/all_to_all | solution.py:101
  28.4 0.2 broadcast_in_dim.28
  28.6 23.5 %all_to_all.21.mine_ref = bf16[8,8,32,384]{3,2,1,0:T(8,128)(2,1)S(1)} all-to-all(bf16[8,8,32,384]{3,2,1,0:T(8,128)(2,1)S(1)} %broadcast_in_dim.28), channel_id=1, replica_groups=mesh['zh'=4,'zl'=2,'xlh'=2,'xll'=2,'yh'=4,'yl'=2,'xh'=2,'c'=2] {'zl','xl..., dimensions={0} | all-to-all | bytes 3145728 | tf_op jit(solution)/shard_map/all_to_all | solution.py:102
  52.1 5.9 %collective-permute-start = (bf16[8,8,32,384]{3,2,1,0:T(8,128)(2,1)S(1)}, bf16[8,8,32,384]{3,2,1,0:T(8,128)(2,1)}, u32[]{:S(2)}, u32[]{:S(2)}) collective-permute-start(bf16[8,8,32,384]{3,2,1,0:T(8,128)(2,1)S(1)} %all_to_all.21.mine_ref), channel_id=1, source_target_pairs={{0,1},{1,0},{2,3},{3,2},{4,5},{5,4},{6,7},{7,6},{8,9},{9,8},{10,11... | collective-permute-start | bytes 4718600 | tf_op jit(solution)/shard_map/ppermute | solution.py:103
  58.1 0.8 constant_dynamic-slice_fusion.1
  59.0 0.1 pad_add_fusion
  59.0 2.2 %collective-permute-done.other_ref = bf16[8,8,32,384]{3,2,1,0:T(8,128)(2,1)} collective-permute-done((bf16[8,8,32,384]{3,2,1,0:T(8,128)(2,1)S(1)}, bf16[8,8,32,384]{3,2,1,0:T(8,128)(2,1)}, u32[]{:S(2)}, u32[]{:S(2)}) %collective-permute-start) | collective-permute-done | bytes 1572896 | tf_op jit(solution)/shard_map/ppermute | solution.py:103
  61.2 4.2 %shard_map.101 = (bf16[4096,384]{1,0:T(8,128)(2,1)}, bf16[192,384]{1,0:T(8,128)(2,1)S(1)}) custom-call(s32[1]{0:T(128)} %bitcast.2.core_ref, bf16[192,4096]{1,0:T(8,128)(2,1)S(1)} %bitcast.36, bf16[8,8,32,384]{3,2,1,0:T(8,128)(2,1)S(1)} %all_to_all.21.mine_ref, bf16[8,8,32,384]{3,2,1,0:T(8,128)(2,1)} %collective-permute-done.other_ref), custom_call_target="tpu_custom_call" | custom-call | flops 603979776 | bytes 4718592 | tf_op jit(solution)/shard_map/pallas_call | solution.py:80
  65.4 1.8 %collective-permute-start.1 = (bf16[192,256]{1,0:T(8,128)(2,1)S(1)}, bf16[192,256]{1,0:T(8,128)(2,1)S(1)}, u32[]{:S(2)}, u32[]{:S(2)}) collective-permute-start(bf16[192,256]{1,0:T(8,128)(2,1)S(1)} %slice.46), channel_id=1, source_target_pairs={{0,32},{32,64},{64,96},{96,128},{128,160},{160,192},{192,224},{224... | collective-permute-start | bytes 294920 | tf_op jit(solution)/shard_map/ppermute | solution.py:26
  67.3 1.8 %collective-permute-done.1 = bf16[192,256]{1,0:T(8,128)(2,1)S(1)} collective-permute-done((bf16[192,256]{1,0:T(8,128)(2,1)S(1)}, bf16[192,256]{1,0:T(8,128)(2,1)S(1)}, u32[]{:S(2)}, u32[]{:S(2)}) %collective-permute-start.1) | collective-permute-done | bytes 98336 | tf_op jit(solution)/shard_map/ppermute | solution.py:26
  69.1 0.3 fusion.27
  69.4 0.3 fusion.4
  69.7 0.3 multiply_reduce_fusion
  70.0 0.3 fusion.9
  70.3 0.1 multiply_convert_fusion
  70.4 0.2 fusion.14
  70.7 1.3 collective-permute-start.2
  72.0 0.2 convolution_convert_fusion.1
  72.2 7.4 %collective-permute-done.2 = f32[2,192,128]{2,1,0:T(8,128)S(1)} collective-permute-done((f32[2,192,128]{2,1,0:T(8,128)S(1)}, f32[2,192,128]{2,1,0:T(8,128)S(1)}, u32[]{:S(2)}, u32[]{:S(2)}) %collective-permute-start.2) | collective-permute-done | bytes 196640 | tf_op jit(solution)/shard_map/ppermute | solution.py:26
  79.7 1.3 shard_map.102
  81.1 3.7 %collective-permute-start.3 = (bf16[8,8,32,384]{3,2,1,0:T(8,128)(2,1)S(1)}, bf16[8,8,32,384]{3,2,1,0:T(8,128)(2,1)S(1)}, u32[]{:S(2)}, u32[]{:S(2)}) collective-permute-start(bf16[8,8,32,384]{3,2,1,0:T(8,128)(2,1)S(1)} %get-tuple-element.12), channel_id=1, source_target_pairs={{0,1},{1,0},{2,3},{3,2},{4,5},{5,4},{6,7},{7,6},{8,9},{9,8},{10,11... | collective-permute-start | bytes 4718600 | tf_op jit(solution)/shard_map/ppermute | solution.py:178
  84.8 3.0 %collective-permute-done.3 = bf16[8,8,32,384]{3,2,1,0:T(8,128)(2,1)S(1)} collective-permute-done((bf16[8,8,32,384]{3,2,1,0:T(8,128)(2,1)S(1)}, bf16[8,8,32,384]{3,2,1,0:T(8,128)(2,1)S(1)}, u32[]{:S(2)}, u32[]{:S(2)}) %collective-permute-start.3) | collective-permute-done | bytes 1572896 | tf_op jit(solution)/shard_map/ppermute | solution.py:178
  87.8 0.4 add_convert_fusion
  88.3 25.0 %all_to_all.22 = bf16[8,8,32,384]{3,2,1,0:T(8,128)(2,1)S(1)} all-to-all(bf16[8,8,32,384]{3,2,1,0:T(8,128)(2,1)S(1)} %add_convert_fusion), channel_id=1, replica_groups=mesh['zh'=4,'zl'=2,'xlh'=2,'xll'=2,'yh'=4,'yl'=2,'xh'=2,'c'=2] {'zl','xl..., dimensions={0} | all-to-all | bytes 3145728 | tf_op jit(solution)/shard_map/all_to_all | solution.py:183
  113.3 0.2 reduce_sum.41
  113.5 0.7 reshape.37
  114.2 15.2 %all-to-all-start.3 = ((bf16[64,4,384]{2,1,0:T(4,128)(2,1)}), bf16[64,4,384]{2,1,0:T(4,128)(2,1)S(1)}, u32[]{:S(2)}, u32[]{:S(2)}) async-start(bf16[64,4,384]{2,1,0:T(4,128)(2,1)} %reshape.37), calls=%async_computation.3 | async-start | bytes 393216 | tf_op jit(solution)/shard_map/all_to_all | solution.py:185
  129.4 0.8 fusion.2
  130.2 4.3 %fusion = bf16[1,192,4096]{2,1,0:T(8,128)(2,1)} fusion(bf16[4096,384]{1,0:T(8,128)(2,1)} %get-tuple-element.10, bf16[192,128]{1,0:T(8,128)(2,1)S(1)} %copy-done.3, bf16[192,128]{1,0:T(8,128)(2,1)S(1)} %get-tuple-element.15, bf16[192,128]{1,0:T(8,128)(2,1)S(1)} %copy-done.5), kind=kOutput, calls=%fused_computation.1 | convolution fusion | flops 605208576 | bytes 4866048 | tf_op jit(solution)/shard_map/dot_general | solution.py:179
  134.5 11.3 %all-to-all-done.3 = bf16[64,4,384]{2,1,0:T(4,128)(2,1)S(1)} async-done(((bf16[64,4,384]{2,1,0:T(4,128)(2,1)}), bf16[64,4,384]{2,1,0:T(4,128)(2,1)S(1)}, u32[]{:S(2)}, u32[]{:S(2)}) %all-to-all-start.3) | async-done | bytes 196640 | tf_op jit(solution)/shard_map/all_to_all | solution.py:185
  145.9 0.6 fusion.26
  (33 shorter events, 0.2 us)
Async XLA Ops:
  0.6 69.0 %copy-start = (bf16[1,192,128]{2,1,0:T(8,128)(2,1)S(1)}, bf16[1,192,128]{2,1,0:T(8,128)(2,1)}, u32[]{:S(2)}) copy-start(bf16[1,192,128]{2,1,0:T(8,128)(2,1)} %param.11) | copy-start | bytes 147460
  28.6 32.6 %copy-start.1 = (bf16[1,192,4096]{2,1,0:T(8,128)(2,1)S(1)}, bf16[1,192,4096]{2,1,0:T(8,128)(2,1)}, u32[]{:S(2)}) copy-start(bf16[1,192,4096]{2,1,0:T(8,128)(2,1)} %param.6) | copy-start | bytes 4718596
  52.1 9.1 %collective-permute-start = (bf16[8,8,32,384]{3,2,1,0:T(8,128)(2,1)S(1)}, bf16[8,8,32,384]{3,2,1,0:T(8,128)(2,1)}, u32[]{:S(2)}, u32[]{:S(2)}) collective-permute-start(bf16[8,8,32,384]{3,2,1,0:T(8,128)(2,1)S(1)} %all_to_all.21.mine_ref), channel_id=1, source_target_pairs={{0,1},{1,0},{2,3},{3,2},{4,5},{5,4},{6,7},{7,6},{8,9},{9,8},{10,11... | collective-permute-start | bytes 4718600 | tf_op jit(solution)/shard_map/ppermute | solution.py:103
  65.4 3.6 %collective-permute-start.1 = (bf16[192,256]{1,0:T(8,128)(2,1)S(1)}, bf16[192,256]{1,0:T(8,128)(2,1)S(1)}, u32[]{:S(2)}, u32[]{:S(2)}) collective-permute-start(bf16[192,256]{1,0:T(8,128)(2,1)S(1)} %slice.46), channel_id=1, source_target_pairs={{0,32},{32,64},{64,96},{96,128},{128,160},{160,192},{192,224},{224... | collective-permute-start | bytes 294920 | tf_op jit(solution)/shard_map/ppermute | solution.py:26
  67.3 2.7 %copy-start.6 = (bf16[192,128]{1,0:T(8,128)(2,1)}, bf16[192,128]{1,0:T(8,128)(2,1)S(1)}, u32[]{:S(2)}) copy-start(bf16[192,128]{1,0:T(8,128)(2,1)S(1)} %get-tuple-element.18) | copy-start | bytes 147460
  69.1 1.2 copy-start.8
  70.7 8.9 %collective-permute-start.2 = (f32[2,192,128]{2,1,0:T(8,128)S(1)}, f32[2,192,128]{2,1,0:T(8,128)S(1)}, u32[]{:S(2)}, u32[]{:S(2)}) collective-permute-start(f32[2,192,128]{2,1,0:T(8,128)S(1)} %pad_maximum_fusion), channel_id=1, source_target_pairs={{32,0},{64,32},{96,64},{128,96},{160,128},{192,160},{224,192},{256... | collective-permute-start | bytes 589832 | tf_op jit(solution)/shard_map/ppermute | solution.py:26
  72.2 8.9 %copy-start.4 = (bf16[192,128]{1,0:T(8,128)(2,1)}, bf16[192,128]{1,0:T(8,128)(2,1)S(1)}, u32[]{:S(2)}) copy-start(bf16[192,128]{1,0:T(8,128)(2,1)S(1)} %convolution_convert_fusion.1) | copy-start | bytes 147460
  79.7 1.4 copy-start.2
  81.1 6.8 %collective-permute-start.3 = (bf16[8,8,32,384]{3,2,1,0:T(8,128)(2,1)S(1)}, bf16[8,8,32,384]{3,2,1,0:T(8,128)(2,1)S(1)}, u32[]{:S(2)}, u32[]{:S(2)}) collective-permute-start(bf16[8,8,32,384]{3,2,1,0:T(8,128)(2,1)S(1)} %get-tuple-element.12), channel_id=1, source_target_pairs={{0,1},{1,0},{2,3},{3,2},{4,5},{5,4},{6,7},{7,6},{8,9},{9,8},{10,11... | collective-permute-start | bytes 4718600 | tf_op jit(solution)/shard_map/ppermute | solution.py:178
  113.2 16.2 %copy-start.7 = (bf16[192,128]{1,0:T(8,128)(2,1)S(1)}, bf16[192,128]{1,0:T(8,128)(2,1)}, u32[]{:S(2)}) copy-start(bf16[192,128]{1,0:T(8,128)(2,1)} %copy-done.6) | copy-start | bytes 147460
  113.2 16.2 %copy-start.9 = (bf16[192,128]{1,0:T(8,128)(2,1)S(1)}, bf16[192,128]{1,0:T(8,128)(2,1)}, u32[]{:S(2)}) copy-start(bf16[192,128]{1,0:T(8,128)(2,1)} %copy-done.8) | copy-start | bytes 147460
  113.3 17.0 %copy-start.3 = (bf16[192,128]{1,0:T(8,128)(2,1)S(1)}, bf16[192,128]{1,0:T(8,128)(2,1)}, u32[]{:S(2)}) copy-start(bf16[192,128]{1,0:T(8,128)(2,1)} %copy-done.2) | copy-start | bytes 147460
  113.3 17.0 %copy-start.5 = (bf16[192,128]{1,0:T(8,128)(2,1)S(1)}, bf16[192,128]{1,0:T(8,128)(2,1)}, u32[]{:S(2)}) copy-start(bf16[192,128]{1,0:T(8,128)(2,1)} %copy-done.4) | copy-start | bytes 147460
  114.2 31.6 %all-to-all-start.3 = ((bf16[64,4,384]{2,1,0:T(4,128)(2,1)}), bf16[64,4,384]{2,1,0:T(4,128)(2,1)S(1)}, u32[]{:S(2)}, u32[]{:S(2)}) async-start(bf16[64,4,384]{2,1,0:T(4,128)(2,1)} %reshape.37), calls=%async_computation.3 | async-start | bytes 393216 | tf_op jit(solution)/shard_map/all_to_all | solution.py:185

commit v2 on v1

v2 whole, which is shorter than its diff:
```python
import math

import jax
import jax.numpy as jnp
from jax import lax
from jax.experimental import pallas as pl
from jax.experimental.pallas import tpu as pltpu
from jax.sharding import Mesh
from jax.sharding import PartitionSpec as P

FSDP = ("zh", "zl", "xlh", "xll")
DP = ("yh", "yl", "xh", "c")
SIZES = (4, 2, 2, 2, 4, 2, 2, 2)
CUBE = ("zl", "xll", "yl")
SWAP = [(0, 1), (1, 0)]
VMEM = 20 * 1024 * 1024


def fsdp_index(zh, zl, xlh, xll):
    return ((zh * 2 + zl) * 2 + xlh) * 2 + xll


def shifted(block, distance):
    route = [(i - distance, i) for i in range(32) if 0 <= i - distance < 32]
    return lax.ppermute(block, FSDP, route)


def project_kernel(core_ref, tok_ref, mine_ref, other_ref, weight_ref, qkv_ref):
    core = core_ref[0]
    for zl in range(2):
        for xll in range(2):
            for yl in range(2):
                for zh in range(4):
                    for xlh in range(2):
                        row = fsdp_index(zh, zl, xlh, xll) * 128 + yl * 32
                        at = (zl * 2 + xll) * 2 + yl, zh * 2 + xlh
                        here = pl.multiple_of(row + core * 64, 32)
                        there = pl.multiple_of(row + (1 - core) * 64, 32)
                        weight_ref[pl.ds(here, 32), :] = mine_ref[at]
                        weight_ref[pl.ds(there, 32), :] = other_ref[at]
    qkv_ref[...] = jnp.dot(
        tok_ref[...], weight_ref[...], preferred_element_type=jnp.float32
    ).astype(jnp.bfloat16)


def attend_kernel(
    qkv_ref, earlier_ref, query_ids_ref, key_ids_ref, upstream_ref, attn_ref, dq_ref, own_ref, back_ref
):
    tok_count, heads = dq_ref.shape
    scale = 1.0 / math.sqrt(heads)
    query = qkv_ref[:, :heads]
    keys = jnp.concatenate([earlier_ref[:, :heads], qkv_ref[:, heads : 2 * heads]], axis=0)
    values = jnp.concatenate([earlier_ref[:, heads:], qkv_ref[:, 2 * heads :]], axis=0)
    upstream = upstream_ref[...]
    across, over = (((1,), (1,)), ((), ())), (((0,), (0,)), ((), ()))

    def dot(a, b, dims):
        return lax.dot_general(a, b, dims, preferred_element_type=jnp.float32)

    rows = lax.broadcasted_iota(jnp.int32, (tok_count, 2 * tok_count), 0)
    columns = lax.broadcasted_iota(jnp.int32, (tok_count, 2 * tok_count), 1)
    allowed = (columns <= rows + tok_count) & (key_ids_ref[...] == query_ids_ref[...])
    scores = jnp.where(allowed, dot(query, keys, across) * scale, -1e30)
    peak = jnp.max(scores, axis=-1, keepdims=True)
    raised = jnp.where(allowed, jnp.exp(scores - peak), 0.0)
    prob = raised / jnp.sum(raised, axis=-1, keepdims=True)
    prob_b = prob.astype(jnp.bfloat16)
    dprob = dot(upstream, values, across)
    delta = jnp.sum(prob * dprob, axis=-1, keepdims=True)
    dscore = (prob * (dprob - delta) * scale).astype(jnp.bfloat16)
    dk = dot(dscore, query, over)
    dv = dot(prob_b, upstream, over)
    back_ref[:, :heads] = dk[:tok_count].astype(jnp.bfloat16)
    back_ref[:, heads:] = dv[:tok_count].astype(jnp.bfloat16)
    own_ref[:, :heads] = dk[tok_count:]
    own_ref[:, heads:] = dv[tok_count:]
    dq_ref[...] = jnp.dot(dscore, keys, preferred_element_type=jnp.float32).astype(jnp.bfloat16)
    attn_ref[...] = jnp.dot(prob_b, values, preferred_element_type=jnp.float32).astype(jnp.bfloat16)


def term_kernel(core_ref, tok_ref, dq_ref, own_ref, back_ref, mine_ref, other_ref, grad_ref):
    first = core_ref[0] == 0
    heads = dq_ref.shape[1]
    grad_ref[:, :heads] = dq_ref[...]
    grad_ref[:, heads:] = (own_ref[...] + back_ref[...].astype(jnp.float32)).astype(jnp.bfloat16)
    grad = grad_ref[...]
    columns = grad.shape[1]
    low = lax.broadcasted_iota(jnp.int32, (8, 8, columns), 1) < 4
    for zh in range(4):
        for zl in range(2):
            for xlh in range(2):
                for xll in range(2):
                    f = fsdp_index(zh, zl, xlh, xll)
                    term = lax.dot_general(
                        tok_ref[:, f * 128 : (f + 1) * 128],
                        grad,
                        (((0,), (0,)), ((), ())),
                        preferred_element_type=jnp.float32,
                    )
                    by_hi = term.reshape(8, 2, 8, columns)
                    even, odd = by_hi[:, 0], by_hi[:, 1]
                    zero = jnp.where(low, even, pltpu.roll(odd, 4, 1))
                    one = jnp.where(low, pltpu.roll(even, 4, 1), odd)
                    mine = jnp.where(first, zero, one).reshape(4, 2, 8, columns)
                    other = jnp.where(first, one, zero).reshape(4, 2, 8, columns)
                    for yl in range(2):
                        at = (zl * 2 + xll) * 2 + yl, zh * 2 + xlh
                        mine_ref[at] = mine[:, yl].reshape(32, columns).astype(jnp.bfloat16)
                        other_ref[at] = other[:, yl].reshape(32, columns).astype(jnp.bfloat16)


def back_kernel(grad_ref, weight_ref, out_ref):
    out_ref[...] = lax.dot_general(
        grad_ref[...], weight_ref[...], (((1,), (1,)), ((), ())), preferred_element_type=jnp.float32
    ).astype(jnp.bfloat16)


def whole(memory=pltpu.VMEM):
    return pl.BlockSpec(memory_space=memory)


def call(kernel, outs, flops, moved, *args):
    scalar = [whole(pltpu.SMEM if arg.ndim == 1 else pltpu.VMEM) for arg in args]
    return pl.pallas_call(
        kernel,
        out_shape=[jax.ShapeDtypeStruct(shape, dtype) for shape, dtype in outs],
        in_specs=scalar,
        out_specs=[whole() for _ in outs],
        compiler_params=pltpu.CompilerParams(vmem_limit_bytes=VMEM),
        cost_estimate=pl.CostEstimate(flops=flops, bytes_accessed=moved, transcendentals=0),
    )(*args)


def input_gradient(grad, weight, flops, moved):
    depth, columns = weight.shape
    wide = 512
    return pl.pallas_call(
        back_kernel,
        grid=(depth // wide,),
        out_shape=jax.ShapeDtypeStruct((grad.shape[0], depth), jnp.bfloat16),
        in_specs=[
            pl.BlockSpec(grad.shape, lambda i: (0, 0)),
            pl.BlockSpec((wide, columns), lambda i: (i, 0)),
        ],
        out_specs=pl.BlockSpec((grad.shape[0], wide), lambda i: (0, i)),
        compiler_params=pltpu.CompilerParams(vmem_limit_bytes=VMEM),
        cost_estimate=pl.CostEstimate(flops=flops, bytes_accessed=moved, transcendentals=0),
    )(grad, weight)


def local(tokens, segment_ids, w_query, w_key, w_value, grad_out):
    tok_rows = tokens[0]
    tok_count, depth = tok_rows.shape
    heads = w_query.shape[1]
    bf16, f32 = jnp.bfloat16, jnp.float32
    core = lax.axis_index("c")
    core_arg = core.reshape(1).astype(jnp.int32)
    flops, moved = 2 * tok_count * depth * 3 * heads, 3 * 2 * tok_count * depth

    local_weight = jnp.concatenate([w_query, w_key, w_value], axis=1)
    start = core * 64 + lax.axis_index("yl") * 32
    quarter = lax.dynamic_slice_in_dim(local_weight, start, 32, axis=0)
    far = lax.all_to_all(jnp.broadcast_to(quarter, (8,) + quarter.shape), ("zh", "xlh"), 0, 0)
    half = lax.all_to_all(jnp.broadcast_to(far, (8,) + far.shape), CUBE, 0, 0)
    other_half = lax.ppermute(half, "c", SWAP)
    full_weight, qkv_rounded = call(
        project_kernel,
        [((depth, 3 * heads), bf16), ((tok_count, 3 * heads), bf16)],
        flops,
        moved,
        core_arg,
        tok_rows,
        half,
        other_half,
    )

    first_row = lax.axis_index(FSDP) * tok_count
    id_line = segment_ids[0]
    own_ids = lax.dynamic_slice_in_dim(id_line, first_row, tok_count)
    prior_ids = lax.dynamic_slice_in_dim(id_line, jnp.maximum(first_row - tok_count, 0), tok_count)
    prior_ids = jnp.where(first_row > 0, prior_ids, -1)
    attn, query_gradient, own_parts, back_parts = call(
        attend_kernel,
        [
            ((tok_count, heads), bf16),
            ((tok_count, heads), bf16),
            ((tok_count, 2 * heads), f32),
            ((tok_count, 2 * heads), bf16),
        ],
        7 * 4 * tok_count * tok_count * heads,
        12 * tok_count * heads,
        qkv_rounded,
        shifted(qkv_rounded[:, heads:], 1),
        own_ids[:, None],
        jnp.concatenate([prior_ids, own_ids])[None, :],
        grad_out[0],
    )
    returned = shifted(back_parts, -1)

    parts = (8, 8, 32, 3 * heads)
    mine, other, grad_proj = call(
        term_kernel,
        [(parts, bf16), (parts, bf16), ((tok_count, 3 * heads), bf16)],
        flops,
        moved,
        core_arg,
        tok_rows,
        query_gradient,
        own_parts,
        returned,
    )
    swapped = lax.ppermute(other, "c", SWAP)
    grad_input = input_gradient(grad_proj, full_weight, flops, moved)
    swapped, grad_input = lax.optimization_barrier((swapped, grad_input))
    chip = (mine.astype(jnp.float32) + swapped.astype(jnp.float32)).astype(jnp.bfloat16)
    cube = jnp.sum(lax.all_to_all(chip, CUBE, 0, 0).astype(jnp.float32), axis=0)
    rows = cube.astype(jnp.bfloat16).reshape(64, 4, 3 * heads)
    rows = lax.all_to_all(rows, ("zh", "xlh", "yh", "xh"), 0, 0)
    count = math.prod(lax.axis_size(name) for name in FSDP + DP) * tok_count
    grads = jnp.sum(rows.astype(jnp.float32), axis=0) * (1.0 / math.sqrt(count))
    return (
        attn[None],
        grad_input[None],
        grads[:, :heads],
        grads[:, heads : 2 * heads],
        grads[:, 2 * heads :],
    )


def solution(mesh):
    fine = Mesh(mesh.devices.reshape(SIZES), FSDP + DP)
    rows = P(DP, FSDP, None)
    weight = P(FSDP, None)
    gradient = P(FSDP + DP, None)
    return jax.shard_map(
        local,
        mesh=fine,
        in_specs=(rows, P(DP, None), weight, weight, weight, rows),
        out_specs=(rows, rows, gradient, gradient, gradient),
        check_vma=False,
    )
```

time: 147 us -> 148 us (level)
  blocking collectives: 75.5 us -> 108 us
  waiting for transfers between devices: 25.7 us -> 9.49 us
  starting transfers between devices: 28 us -> 13 us
  matrix products: 6.42 us -> 0 us
  Pallas kernels: 5.51 us -> 9.77 us
  local copies, waits for them, and re-layouts: 2.44 us -> 4.49 us
    all_to_all x0 -> x1, blocking collectives: none -> 31.3 us  [local(): rows = lax.all_to_all(rows, ('zh', 'xlh', 'yh', 'xh'), 0, 0)]
    all_to_all x1 -> x0, starting transfers between devices: 15.2 us -> none  [local(): rows = lax.all_to_all(rows, ('zh', 'xlh', 'yh', 'xh'), 0, 0)]
    all_to_all x1 -> x0, waiting for transfers between devices: 11.3 us -> none  [local(): rows = lax.all_to_all(rows, ('zh', 'xlh', 'yh', 'xh'), 0, 0)]
    dot_general x7 -> x0, matrix products: 6.42 us -> none  [the longest x1 4.28 us: local(): lax.dot_general(grad_proj, full_weight, (((1,), (1,)), ((), ())), preferr...]
    pallas_call x2 -> x4, Pallas kernels: 5.51 us -> 9.77 us  [the longest x3 5.55 us: call(): pl.pallas_call(kernel, out_shape=[jax.ShapeDtypeStruct(shape, dtype) for...]
    unnamed x20 -> x8, local copies, waits for them, and re-layouts: 0.05 us -> 3.53 us
    ppermute x1, waiting for transfers between devices: 3.01 us -> 0.01 us  [local(): swapped = lax.ppermute(other, 'c', SWAP)]
    ppermute x2, waiting for transfers between devices: 9.19 us -> 7.19 us  [shifted(): return lax.ppermute(block, FSDP, route)]
  transfers between devices with their start and end apart: 5 -> 4, of which waited for: 5 -> 3; matrix products, arithmetic and copies ran while one was open for 4% -> 1% of each run, Pallas kernels for 0% -> 3%
where the time goes in v2:
time: 148 us; the launch traced here: 147 us
  blocking collectives  108 us (73%)
  starting transfers between devices  13 us (9%)
  Pallas kernels  9.77 us (7%)
  waiting for transfers between devices  9.49 us (6%)
  local copies, waits for them, and re-layouts  4.49 us (3%)
  other arithmetic  2.39 us (2%)
    all_to_all x1, blocking collectives, local(): rows = lax.all_to_all(rows, ('zh', 'xlh', 'yh', 'xh'), 0, 0)  31.3 us
    all_to_all x1, blocking collectives, local(): lax.all_to_all(jnp.broadcast_to(quarter, (8,) + quarter.shape), ('zh', 'x...  27 us
    all_to_all x1, blocking collectives, local(): cube = jnp.sum(lax.all_to_all(chip, CUBE, 0, 0).astype(jnp.float32), axis=0)  25.7 us
    all_to_all x1, blocking collectives, local(): half = lax.all_to_all(jnp.broadcast_to(far, (8,) + far.shape), CUBE, 0, 0)  23.5 us
    ppermute x2, waiting for transfers between devices, shifted(): return lax.ppermute(block, FSDP, route)  7.19 us
    ppermute x1, starting transfers between devices, local(): other_half = lax.ppermute(half, 'c', SWAP)  5.95 us
    pallas_call x3, Pallas kernels, call(): pl.pallas_call(kernel, out_shape=[jax.ShapeDtypeStruct(shape, dtype) for...  5.55 us
    pallas_call x1, Pallas kernels, input_gradient(): pl.pallas_call(back_kernel, grid=(depth // wide,), out_shape=jax.ShapeDty...  4.22 us
  transfers between devices with their start and end apart: 4, of which 3 were waited for; matrix products, arithmetic and copies ran while one was open for 1% of the time, Pallas kernels for 3%

profile of v2, /device:TPU:1, one launch (start us, length us, event | category | flops | bytes accessed | tf_op | source)
XLA Modules:
  0.0 147.5 jit_solution(3560589927179066420)
XLA Ops:
  0.6 0.7 fusion.1
  1.4 27.0 %all_to_all.20 = bf16[8,32,384]{2,1,0:T(8,128)(2,1)S(1)} all-to-all(bf16[8,32,384]{2,1,0:T(8,128)(2,1)S(1)} %broadcast_in_dim.22), channel_id=1, replica_groups=mesh['zh'=4,'zl'=2,'xlh'=2,'xll'=2,'yh'=4,'yl'=2,'xh'=2,'c'=2] {'zh','xlh'}, dimensions={0} | all-to-all | bytes 393216 | tf_op jit(solution)/shard_map/all_to_all | solution.py:163
  28.4 0.2 broadcast_in_dim.23
  28.6 0.0 copy-start.2
  28.6 23.5 %all_to_all.21.mine_ref = bf16[8,8,32,384]{3,2,1,0:T(8,128)(2,1)S(1)} all-to-all(bf16[8,8,32,384]{3,2,1,0:T(8,128)(2,1)S(1)} %broadcast_in_dim.23), channel_id=1, replica_groups=mesh['zh'=4,'zl'=2,'xlh'=2,'xll'=2,'yh'=4,'yl'=2,'xh'=2,'c'=2] {'zl','xl..., dimensions={0} | all-to-all | bytes 3145728 | tf_op jit(solution)/shard_map/all_to_all | solution.py:164
  52.1 5.9 %collective-permute-start = (bf16[8,8,32,384]{3,2,1,0:T(8,128)(2,1)S(1)}, bf16[8,8,32,384]{3,2,1,0:T(8,128)(2,1)}, u32[]{:S(2)}, u32[]{:S(2)}) collective-permute-start(bf16[8,8,32,384]{3,2,1,0:T(8,128)(2,1)S(1)} %all_to_all.21.mine_ref), channel_id=1, source_target_pairs={{0,1},{1,0},{2,3},{3,2},{4,5},{5,4},{6,7},{7,6},{8,9},{9,8},{10,11... | collective-permute-start | bytes 4718600 | tf_op jit(solution)/shard_map/ppermute | solution.py:165
  58.1 0.8 broadcast_select_fusion
  58.9 2.3 %collective-permute-done.other_ref = bf16[8,8,32,384]{3,2,1,0:T(8,128)(2,1)} collective-permute-done((bf16[8,8,32,384]{3,2,1,0:T(8,128)(2,1)S(1)}, bf16[8,8,32,384]{3,2,1,0:T(8,128)(2,1)}, u32[]{:S(2)}, u32[]{:S(2)}) %collective-permute-start) | collective-permute-done | bytes 1572896 | tf_op jit(solution)/shard_map/ppermute | solution.py:165
  61.2 0.0 copy-done.2
  61.2 2.7 %shard_map.101 = (bf16[4096,384]{1,0:T(8,128)(2,1)S(1)}, bf16[192,384]{1,0:T(8,128)(2,1)S(1)}) custom-call(s32[1]{0:T(128)} %bitcast.core_ref, bf16[192,4096]{1,0:T(8,128)(2,1)S(1)} %bitcast.8, bf16[8,8,32,384]{3,2,1,0:T(8,128)(2,1)S(1)} %all_to_all.21.mine_ref, bf16[8,8,32,384]{3,2,1,0:T(8,128)(2,1)} %collective-permute-done.other_ref), custom_call_target="tpu_custom_call" | custom-call | flops 603979776 | bytes 4718592 | tf_op jit(solution)/shard_map/pallas_call | solution.py:124
  63.9 0.0 copy-start
  63.9 1.6 %copy-done = bf16[4096,384]{1,0:T(8,128)(2,1)} copy-done((bf16[4096,384]{1,0:T(8,128)(2,1)}, bf16[4096,384]{1,0:T(8,128)(2,1)S(1)}, u32[]{:S(2)}) %copy-start) | copy-done | bytes 3145752
  65.6 1.8 %collective-permute-start.1 = (bf16[192,256]{1,0:T(8,128)(2,1)S(1)}, bf16[192,256]{1,0:T(8,128)(2,1)S(1)}, u32[]{:S(2)}, u32[]{:S(2)}) collective-permute-start(bf16[192,256]{1,0:T(8,128)(2,1)S(1)} %slice.12), channel_id=1, source_target_pairs={{0,32},{32,64},{64,96},{96,128},{128,160},{160,192},{192,224},{224... | collective-permute-start | bytes 294920 | tf_op jit(solution)/shard_map/ppermute | solution.py:25
  67.4 0.1 pad_add_fusion
  67.5 0.1 copy.17.query_ids_ref
  67.6 1.6 %collective-permute-done.1.earlier_ref = bf16[192,256]{1,0:T(8,128)(2,1)S(1)} collective-permute-done((bf16[192,256]{1,0:T(8,128)(2,1)S(1)}, bf16[192,256]{1,0:T(8,128)(2,1)S(1)}, u32[]{:S(2)}, u32[]{:S(2)}) %collective-permute-start.1) | collective-permute-done | bytes 98336 | tf_op jit(solution)/shard_map/ppermute | solution.py:25
  69.2 0.0 copy-done.3
  69.2 1.5 %shard_map.102 = (bf16[192,128]{1,0:T(8,128)(2,1)}, bf16[192,128]{1,0:T(8,128)(2,1)S(1)}, f32[192,256]{1,0:T(8,128)S(1)}, bf16[192,256]{1,0:T(8,128)(2,1)S(1)}) custom-call(bf16[192,384]{1,0:T(8,128)(2,1)S(1)} %get-tuple-element.16.qkv_ref, bf16[192,256]{1,0:T(8,128)(2,1)S(1)} %collective-permute-done.1.earlier_ref, s32[192,1]{1,0:T(8,128)S(1)} %copy.17.query_ids_ref, ...), custom_call_target="tpu_custom_call" | custom-call | flops 132120576 | bytes 294912 | tf_op jit(solution)/shard_map/pallas_call | solution.py:124
  70.7 1.3 collective-permute-start.2
  72.0 5.6 %collective-permute-done.2.back_ref = bf16[192,256]{1,0:T(8,128)(2,1)S(1)} collective-permute-done((bf16[192,256]{1,0:T(8,128)(2,1)S(1)}, bf16[192,256]{1,0:T(8,128)(2,1)S(1)}, u32[]{:S(2)}, u32[]{:S(2)}) %collective-permute-start.2) | collective-permute-done | bytes 98336 | tf_op jit(solution)/shard_map/ppermute | solution.py:25
  77.6 1.4 shard_map.103
  79.0 4.0 %collective-permute-start.3 = (bf16[8,8,32,384]{3,2,1,0:T(8,128)(2,1)S(1)}, bf16[8,8,32,384]{3,2,1,0:T(8,128)(2,1)S(1)}, u32[]{:S(2)}, u32[]{:S(2)}) collective-permute-start(bf16[8,8,32,384]{3,2,1,0:T(8,128)(2,1)S(1)} %get-tuple-element.21), channel_id=1, source_target_pairs={{0,1},{1,0},{2,3},{3,2},{4,5},{5,4},{6,7},{7,6},{8,9},{9,8},{10,11... | collective-permute-start | bytes 4718600 | tf_op jit(solution)/shard_map/ppermute | solution.py:212
  83.0 0.0 copy-start.1
  83.0 1.9 %copy-done.1 = bf16[4096,384]{1,0:T(8,128)(2,1)S(1)} copy-done((bf16[4096,384]{1,0:T(8,128)(2,1)S(1)}, bf16[4096,384]{1,0:T(8,128)(2,1)}, u32[]{:S(2)}) %copy-start.1) | copy-done | bytes 3145752
  84.9 4.2 %shard_map.104 = bf16[192,4096]{1,0:T(8,128)(2,1)} custom-call(bf16[192,384]{1,0:T(8,128)(2,1)S(1)} %get-tuple-element.22.grad_ref, bf16[4096,384]{1,0:T(8,128)(2,1)S(1)} %copy-done.1), custom_call_target="tpu_custom_call" | custom-call | flops 603979776 | bytes 4718592 | tf_op jit(solution)/shard_map/pallas_call | solution.py:137
  89.1 0.0 collective-permute-done.3
  89.1 0.5 add_convert_fusion
  89.5 25.7 %all_to_all.22 = bf16[8,8,32,384]{3,2,1,0:T(8,128)(2,1)S(1)} all-to-all(bf16[8,8,32,384]{3,2,1,0:T(8,128)(2,1)S(1)} %add_convert_fusion), channel_id=1, replica_groups=mesh['zh'=4,'zl'=2,'xlh'=2,'xll'=2,'yh'=4,'yl'=2,'xh'=2,'c'=2] {'zl','xl..., dimensions={0} | all-to-all | bytes 3145728 | tf_op jit(solution)/shard_map/all_to_all | solution.py:216
  115.2 0.2 reduce_sum.21
  115.5 0.1 reshape.23
  115.5 31.3 %all_to_all.23 = bf16[64,4,384]{2,1,0:T(4,128)(2,1)S(1)} all-to-all(bf16[64,4,384]{2,1,0:T(4,128)(2,1)S(1)} %reshape.23), channel_id=1, replica_groups=mesh['zh'=4,'zl'=2,'xlh'=2,'xll'=2,'yh'=4,'yl'=2,'xh'=2,'c'=2] {'zh','xl..., dimensions={0} | all-to-all | bytes 393216 | tf_op jit(solution)/shard_map/all_to_all | solution.py:218
  146.9 0.6 fusion.2
  (6 shorter events, 0.1 us)
Async XLA Ops:
  28.6 32.6 %copy-start.2 = (bf16[1,192,4096]{2,1,0:T(8,128)(2,1)S(1)}, bf16[1,192,4096]{2,1,0:T(8,128)(2,1)}, u32[]{:S(2)}) copy-start(bf16[1,192,4096]{2,1,0:T(8,128)(2,1)} %param.6) | copy-start | bytes 4718596
  52.1 9.1 %collective-permute-start = (bf16[8,8,32,384]{3,2,1,0:T(8,128)(2,1)S(1)}, bf16[8,8,32,384]{3,2,1,0:T(8,128)(2,1)}, u32[]{:S(2)}, u32[]{:S(2)}) collective-permute-start(bf16[8,8,32,384]{3,2,1,0:T(8,128)(2,1)S(1)} %all_to_all.21.mine_ref), channel_id=1, source_target_pairs={{0,1},{1,0},{2,3},{3,2},{4,5},{5,4},{6,7},{7,6},{8,9},{9,8},{10,11... | collective-permute-start | bytes 4718600 | tf_op jit(solution)/shard_map/ppermute | solution.py:165
  61.2 8.0 %copy-start.3 = (bf16[1,192,128]{2,1,0:T(8,128)(2,1)S(1)}, bf16[1,192,128]{2,1,0:T(8,128)(2,1)}, u32[]{:S(2)}) copy-start(bf16[1,192,128]{2,1,0:T(8,128)(2,1)} %param.11) | copy-start | bytes 147460
  63.9 1.6 %copy-start = (bf16[4096,384]{1,0:T(8,128)(2,1)}, bf16[4096,384]{1,0:T(8,128)(2,1)S(1)}, u32[]{:S(2)}) copy-start(bf16[4096,384]{1,0:T(8,128)(2,1)S(1)} %get-tuple-element.23.weight_ref) | copy-start | bytes 9437188
  65.6 3.6 %collective-permute-start.1 = (bf16[192,256]{1,0:T(8,128)(2,1)S(1)}, bf16[192,256]{1,0:T(8,128)(2,1)S(1)}, u32[]{:S(2)}, u32[]{:S(2)}) collective-permute-start(bf16[192,256]{1,0:T(8,128)(2,1)S(1)} %slice.12), channel_id=1, source_target_pairs={{0,32},{32,64},{64,96},{96,128},{128,160},{160,192},{192,224},{224... | collective-permute-start | bytes 294920 | tf_op jit(solution)/shard_map/ppermute | solution.py:25
  70.7 6.9 %collective-permute-start.2 = (bf16[192,256]{1,0:T(8,128)(2,1)S(1)}, bf16[192,256]{1,0:T(8,128)(2,1)S(1)}, u32[]{:S(2)}, u32[]{:S(2)}) collective-permute-start(bf16[192,256]{1,0:T(8,128)(2,1)S(1)} %get-tuple-element.20), channel_id=1, source_target_pairs={{32,0},{64,32},{96,64},{128,96},{160,128},{192,160},{224,192},{256... | collective-permute-start | bytes 294920 | tf_op jit(solution)/shard_map/ppermute | solution.py:25
  79.0 10.1 %collective-permute-start.3 = (bf16[8,8,32,384]{3,2,1,0:T(8,128)(2,1)S(1)}, bf16[8,8,32,384]{3,2,1,0:T(8,128)(2,1)S(1)}, u32[]{:S(2)}, u32[]{:S(2)}) collective-permute-start(bf16[8,8,32,384]{3,2,1,0:T(8,128)(2,1)S(1)} %get-tuple-element.21), channel_id=1, source_target_pairs={{0,1},{1,0},{2,3},{3,2},{4,5},{5,4},{6,7},{7,6},{8,9},{9,8},{10,11... | collective-permute-start | bytes 4718600 | tf_op jit(solution)/shard_map/ppermute | solution.py:212
  83.0 1.9 %copy-start.1 = (bf16[4096,384]{1,0:T(8,128)(2,1)S(1)}, bf16[4096,384]{1,0:T(8,128)(2,1)}, u32[]{:S(2)}) copy-start(bf16[4096,384]{1,0:T(8,128)(2,1)} %copy-done) | copy-start | bytes 9437188

commit v3 on v2

--- a/solution.py
+++ b/solution.py
@@ -11,13 +11,35 @@
 FSDP = ("zh", "zl", "xlh", "xll")
 DP = ("yh", "yl", "xh", "c")
 SIZES = (4, 2, 2, 2, 4, 2, 2, 2)
-CUBE = ("zl", "xll", "yl")
 SWAP = [(0, 1), (1, 0)]
 VMEM = 20 * 1024 * 1024
 
 
 def fsdp_index(zh, zl, xlh, xll):
     return ((zh * 2 + zl) * 2 + xlh) * 2 + xll
+
+
+def cubes():
+    def index(z, x, y, core):
+        x_hi = x // 4
+        fsdp = z * 4 + x % 4
+        return ((fsdp * 8 + y) * 2 + x_hi) * 2 + core
+
+    groups = []
+    for core in range(2):
+        for corner in range(64):
+            low = [2 * (corner // 16) + core, 2 * (corner // 4 % 4) + core, 2 * (corner % 4) + core]
+            members = []
+            for bits in range(8):
+                want = (bits // 4, bits // 2 % 2, bits % 2)
+                z, x, y = ((a + (a + b) % 2) % 8 for a, b in zip(low, want))
+                members.append(index(z, x, y, core))
+            groups.append(members)
+    return groups
+
+
+def cube_exchange(block):
+    return lax.all_to_all(block, FSDP + DP, 0, 0, axis_index_groups=cubes())
 
 
 def shifted(block, distance):
@@ -25,22 +47,32 @@
     return lax.ppermute(block, FSDP, route)
 
 
-def project_kernel(core_ref, tok_ref, mine_ref, other_ref, weight_ref, qkv_ref):
+def project_kernel(core_ref, tok_ref, mine_ref, other_ref, weight_ref, qkv_ref, *scratch):
     core = core_ref[0]
-    for zl in range(2):
-        for xll in range(2):
-            for yl in range(2):
-                for zh in range(4):
-                    for xlh in range(2):
-                        row = fsdp_index(zh, zl, xlh, xll) * 128 + yl * 32
+    total, copies = None, []
+    for zh in range(4):
+        part_ref, done = scratch[zh], scratch[4].at[zh]
+        for zl in range(2):
+            for xlh in range(2):
+                for xll in range(2):
+                    for yl in range(2):
+                        row = fsdp_index(0, zl, xlh, xll) * 128 + yl * 32
                         at = (zl * 2 + xll) * 2 + yl, zh * 2 + xlh
                         here = pl.multiple_of(row + core * 64, 32)
                         there = pl.multiple_of(row + (1 - core) * 64, 32)
-                        weight_ref[pl.ds(here, 32), :] = mine_ref[at]
-                        weight_ref[pl.ds(there, 32), :] = other_ref[at]
-    qkv_ref[...] = jnp.dot(
-        tok_ref[...], weight_ref[...], preferred_element_type=jnp.float32
-    ).astype(jnp.bfloat16)
+                        part_ref[pl.ds(here, 32), :] = mine_ref[at]
+                        part_ref[pl.ds(there, 32), :] = other_ref[at]
+        rows = part_ref.shape[0]
+        copy = pltpu.make_async_copy(part_ref, weight_ref.at[pl.ds(zh * rows, rows), :], done)
+        copy.start()
+        copies.append(copy)
+        term = jnp.dot(
+            tok_ref[:, zh * rows : (zh + 1) * rows], part_ref[...], preferred_element_type=jnp.float32
+        )
+        total = term if total is None else total + term
+    qkv_ref[...] = total.astype(jnp.bfloat16)
+    for copy in copies:
+        copy.wait()
 
 
 def attend_kernel(
@@ -109,43 +141,48 @@
                         other_ref[at] = other[:, yl].reshape(32, columns).astype(jnp.bfloat16)
 
 
-def back_kernel(grad_ref, weight_ref, out_ref):
-    out_ref[...] = lax.dot_general(
-        grad_ref[...], weight_ref[...], (((1,), (1,)), ((), ())), preferred_element_type=jnp.float32
-    ).astype(jnp.bfloat16)
+def back_kernel(grad_ref, weight_ref, out_ref, *scratch):
+    grad, count = grad_ref[...], 4
+    parts, blocks, arrived, left = scratch[:4], scratch[4:8], scratch[8], scratch[9]
+    rows = weight_ref.shape[0] // count
+    fetches = [
+        pltpu.make_async_copy(weight_ref.at[pl.ds(i * rows, rows), :], parts[i], arrived.at[i])
+        for i in range(count)
+    ]
+    stores = [
+        pltpu.make_async_copy(blocks[i], out_ref.at[:, pl.ds(i * rows, rows)], left.at[i])
+        for i in range(count)
+    ]
+    for fetch in fetches:
+        fetch.start()
+    for i in range(count):
+        fetches[i].wait()
+        blocks[i][...] = lax.dot_general(
+            grad, parts[i][...], (((1,), (1,)), ((), ())), preferred_element_type=jnp.float32
+        ).astype(jnp.bfloat16)
+        stores[i].start()
+    for store in stores:
+        store.wait()
 
 
 def whole(memory=pltpu.VMEM):
     return pl.BlockSpec(memory_space=memory)
 
 
-def call(kernel, outs, flops, moved, *args):
-    scalar = [whole(pltpu.SMEM if arg.ndim == 1 else pltpu.VMEM) for arg in args]
+def call(kernel, outs, flops, moved, *args, far_args=(), far_outs=(), scratch=()):
+    def space(i, array, far):
+        return whole(pl.ANY if i in far else pltpu.SMEM if array.ndim == 1 else pltpu.VMEM)
+
+    shapes = [jax.ShapeDtypeStruct(shape, dtype) for shape, dtype in outs]
     return pl.pallas_call(
         kernel,
-        out_shape=[jax.ShapeDtypeStruct(shape, dtype) for shape, dtype in outs],
-        in_specs=scalar,
-        out_specs=[whole() for _ in outs],
+        out_shape=shapes,
+        in_specs=[space(i, arg, far_args) for i, arg in enumerate(args)],
+        out_specs=[space(i, shape, far_outs) for i, shape in enumerate(shapes)],
+        scratch_shapes=list(scratch),
         compiler_params=pltpu.CompilerParams(vmem_limit_bytes=VMEM),
         cost_estimate=pl.CostEstimate(flops=flops, bytes_accessed=moved, transcendentals=0),
     )(*args)
-
-
-def input_gradient(grad, weight, flops, moved):
-    depth, columns = weight.shape
-    wide = 512
-    return pl.pallas_call(
-        back_kernel,
-        grid=(depth // wide,),
-        out_shape=jax.ShapeDtypeStruct((grad.shape[0], depth), jnp.bfloat16),
-        in_specs=[
-            pl.BlockSpec(grad.shape, lambda i: (0, 0)),
-            pl.BlockSpec((wide, columns), lambda i: (i, 0)),
-        ],
-        out_specs=pl.BlockSpec((grad.shape[0], wide), lambda i: (0, i)),
-        compiler_params=pltpu.CompilerParams(vmem_limit_bytes=VMEM),
-        cost_estimate=pl.CostEstimate(flops=flops, bytes_accessed=moved, transcendentals=0),
-    )(grad, weight)
 
 
 def local(tokens, segment_ids, w_query, w_key, w_value, grad_out):
@@ -157,11 +194,14 @@
     core_arg = core.reshape(1).astype(jnp.int32)
     flops, moved = 2 * tok_count * depth * 3 * heads, 3 * 2 * tok_count * depth
 
+    weight_part = pltpu.VMEM((depth // 4, 3 * heads), bf16)
+    tok_part = pltpu.VMEM((tok_count, depth // 4), bf16)
+
     local_weight = jnp.concatenate([w_query, w_key, w_value], axis=1)
     start = core * 64 + lax.axis_index("yl") * 32
     quarter = lax.dynamic_slice_in_dim(local_weight, start, 32, axis=0)
     far = lax.all_to_all(jnp.broadcast_to(quarter, (8,) + quarter.shape), ("zh", "xlh"), 0, 0)
-    half = lax.all_to_all(jnp.broadcast_to(far, (8,) + far.shape), CUBE, 0, 0)
+    half = cube_exchange(jnp.broadcast_to(far, (8,) + far.shape))
     other_half = lax.ppermute(half, "c", SWAP)
     full_weight, qkv_rounded = call(
         project_kernel,
@@ -172,6 +212,8 @@
         tok_rows,
         half,
         other_half,
+        far_outs=(0,),
+        scratch=[weight_part] * 4 + [pltpu.SemaphoreType.DMA((4,))],
     )
 
     first_row = lax.axis_index(FSDP) * tok_count
@@ -210,10 +252,20 @@
         returned,
     )
     swapped = lax.ppermute(other, "c", SWAP)
-    grad_input = input_gradient(grad_proj, full_weight, flops, moved)
+    (grad_input,) = call(
+        back_kernel,
+        [((tok_count, depth), bf16)],
+        flops,
+        moved,
+        grad_proj,
+        full_weight,
+        far_args=(1,),
+        far_outs=(0,),
+        scratch=[weight_part] * 4 + [tok_part] * 4 + [pltpu.SemaphoreType.DMA((4,))] * 2,
+    )
     swapped, grad_input = lax.optimization_barrier((swapped, grad_input))
     chip = (mine.astype(jnp.float32) + swapped.astype(jnp.float32)).astype(jnp.bfloat16)
-    cube = jnp.sum(lax.all_to_all(chip, CUBE, 0, 0).astype(jnp.float32), axis=0)
+    cube = jnp.sum(cube_exchange(chip).astype(jnp.float32), axis=0)
     rows = cube.astype(jnp.bfloat16).reshape(64, 4, 3 * heads)
     rows = lax.all_to_all(rows, ("zh", "xlh", "yh", "xh"), 0, 0)
     count = math.prod(lax.axis_size(name) for name in FSDP + DP) * tok_count

time: 148 us -> 140 us (0.946)
  starting transfers between devices: 13 us -> 7.66 us
  blocking collectives: 108 us -> 106 us
    ppermute x1, starting transfers between devices: 5.95 us -> 1.91 us  [local(): other_half = lax.ppermute(half, 'c', SWAP)]
    all_to_all x1, blocking collectives: 31.3 us -> 29.4 us  [local(): rows = lax.all_to_all(rows, ('zh', 'xlh', 'yh', 'xh'), 0, 0)]
  transfers between devices with their start and end apart: 4 -> 4, of which waited for: 3 -> 3; matrix products, arithmetic and copies ran while one was open for 1% -> 1% of each run, Pallas kernels for 3% -> 2%
where the time goes in v3:
time: 140 us
  blocking collectives  106 us (76%)
  waiting for transfers between devices  10 us (7%)
  Pallas kernels  8.8 us (6%)
  starting transfers between devices  7.66 us (5%)
  local copies, waits for them, and re-layouts  4.49 us (3%)
  other arithmetic  2.39 us (2%)
    all_to_all x2, blocking collectives, cube_exchange(): return lax.all_to_all(block, FSDP + DP, 0, 0, axis_index_groups=cubes())  49.2 us
    all_to_all x1, blocking collectives, local(): rows = lax.all_to_all(rows, ('zh', 'xlh', 'yh', 'xh'), 0, 0)  29.4 us
    all_to_all x1, blocking collectives, local(): lax.all_to_all(jnp.broadcast_to(quarter, (8,) + quarter.shape), ('zh', 'x...  27 us
    pallas_call x4, Pallas kernels, call(): pl.pallas_call(kernel, out_shape=shapes, in_specs=[space(i, arg, far_args...  8.8 us
    ppermute x2, waiting for transfers between devices, shifted(): return lax.ppermute(block, FSDP, route)  7.35 us
    unnamed x8, local copies, waits for them, and re-layouts  3.53 us
    ppermute x1, starting transfers between devices, local(): swapped = lax.ppermute(other, 'c', SWAP)  3.18 us
  transfers between devices with their start and end apart: 4, of which 3 were waited for; matrix products, arithmetic and copies ran while one was open for 1% of the time, Pallas kernels for 2%

profile of v3, /device:TPU:1, one launch (start us, length us, event | category | flops | bytes accessed | tf_op | source)
XLA Modules:
  0.0 139.7 jit_solution(4483119416535899372)
XLA Ops:
  0.6 0.7 fusion.1
  1.4 27.0 %all_to_all.20 = bf16[8,32,384]{2,1,0:T(8,128)(2,1)S(1)} all-to-all(bf16[8,32,384]{2,1,0:T(8,128)(2,1)S(1)} %broadcast_in_dim.22), channel_id=1, replica_groups=mesh['zh'=4,'zl'=2,'xlh'=2,'xll'=2,'yh'=4,'yl'=2,'xh'=2,'c'=2] {'zh','xlh'}, dimensions={0} | all-to-all | bytes 393216 | tf_op jit(solution)/shard_map/all_to_all | solution.py:203
  28.4 0.2 broadcast_in_dim.23
  28.6 0.0 copy-start.2
  28.6 24.3 %all_to_all.21.mine_ref = bf16[8,8,32,384]{3,2,1,0:T(8,128)(2,1)S(1)} all-to-all(bf16[8,8,32,384]{3,2,1,0:T(8,128)(2,1)S(1)} %broadcast_in_dim.23), channel_id=1, replica_groups={{0,4,32,36,128,132,160,164},{8,12,40,44,136,140,168,172},{16,20,48,52,1..., dimensions={0} | all-to-all | bytes 3145728 | tf_op jit(solution)/shard_map/all_to_all | solution.py:42
  52.9 1.9 %collective-permute-start = (bf16[8,8,32,384]{3,2,1,0:T(8,128)(2,1)S(1)}, bf16[8,8,32,384]{3,2,1,0:T(8,128)(2,1)}, u32[]{:S(2)}, u32[]{:S(2)}) collective-permute-start(bf16[8,8,32,384]{3,2,1,0:T(8,128)(2,1)S(1)} %all_to_all.21.mine_ref), channel_id=1, source_target_pairs={{0,1},{1,0},{2,3},{3,2},{4,5},{5,4},{6,7},{7,6},{8,9},{9,8},{10,11... | collective-permute-start | bytes 4718600 | tf_op jit(solution)/shard_map/ppermute | solution.py:205
  54.8 0.8 broadcast_select_fusion
  55.6 2.7 %collective-permute-done.other_ref = bf16[8,8,32,384]{3,2,1,0:T(8,128)(2,1)} collective-permute-done((bf16[8,8,32,384]{3,2,1,0:T(8,128)(2,1)S(1)}, bf16[8,8,32,384]{3,2,1,0:T(8,128)(2,1)}, u32[]{:S(2)}, u32[]{:S(2)}) %collective-permute-start) | collective-permute-done | bytes 1572896 | tf_op jit(solution)/shard_map/ppermute | solution.py:205
  58.3 0.0 copy-done.2
  58.3 3.2 %shard_map.101 = (bf16[4096,384]{1,0:T(8,128)(2,1)S(1)}, bf16[192,384]{1,0:T(8,128)(2,1)S(1)}) custom-call(s32[1]{0:T(128)} %bitcast.core_ref, bf16[192,4096]{1,0:T(8,128)(2,1)S(1)} %bitcast.8, bf16[8,8,32,384]{3,2,1,0:T(8,128)(2,1)S(1)} %all_to_all.21.mine_ref, bf16[8,8,32,384]{3,2,1,0:T(8,128)(2,1)} %collective-permute-done.other_ref), custom_call_target="tpu_custom_call" | custom-call | flops 603979776 | bytes 4718592 | tf_op jit(solution)/shard_map/pallas_call | solution.py:177
  61.5 0.0 copy-start
  61.5 1.6 %copy-done = bf16[4096,384]{1,0:T(8,128)(2,1)} copy-done((bf16[4096,384]{1,0:T(8,128)(2,1)}, bf16[4096,384]{1,0:T(8,128)(2,1)S(1)}, u32[]{:S(2)}) %copy-start) | copy-done | bytes 3145752
  63.2 1.3 collective-permute-start.1
  64.5 0.1 pad_add_fusion
  64.5 0.1 copy.17.query_ids_ref
  64.7 2.1 %collective-permute-done.1.earlier_ref = bf16[192,256]{1,0:T(8,128)(2,1)S(1)} collective-permute-done((bf16[192,256]{1,0:T(8,128)(2,1)S(1)}, bf16[192,256]{1,0:T(8,128)(2,1)S(1)}, u32[]{:S(2)}, u32[]{:S(2)}) %collective-permute-start.1) | collective-permute-done | bytes 98336 | tf_op jit(solution)/shard_map/ppermute | solution.py:47
  66.7 0.0 copy-done.3
  66.7 1.5 %shard_map.102 = (bf16[192,128]{1,0:T(8,128)(2,1)}, bf16[192,128]{1,0:T(8,128)(2,1)S(1)}, f32[192,256]{1,0:T(8,128)S(1)}, bf16[192,256]{1,0:T(8,128)(2,1)S(1)}) custom-call(bf16[192,384]{1,0:T(8,128)(2,1)S(1)} %get-tuple-element.16.qkv_ref, bf16[192,256]{1,0:T(8,128)(2,1)S(1)} %collective-permute-done.1.earlier_ref, s32[192,1]{1,0:T(8,128)S(1)} %copy.17.query_ids_ref, ...), custom_call_target="tpu_custom_call" | custom-call | flops 132120576 | bytes 294912 | tf_op jit(solution)/shard_map/pallas_call | solution.py:177
  68.2 1.3 collective-permute-start.2
  69.5 5.3 %collective-permute-done.2.back_ref = bf16[192,256]{1,0:T(8,128)(2,1)S(1)} collective-permute-done((bf16[192,256]{1,0:T(8,128)(2,1)S(1)}, bf16[192,256]{1,0:T(8,128)(2,1)S(1)}, u32[]{:S(2)}, u32[]{:S(2)}) %collective-permute-start.2) | collective-permute-done | bytes 98336 | tf_op jit(solution)/shard_map/ppermute | solution.py:47
  74.8 1.4 shard_map.103
  76.1 3.2 %collective-permute-start.3 = (bf16[8,8,32,384]{3,2,1,0:T(8,128)(2,1)S(1)}, bf16[8,8,32,384]{3,2,1,0:T(8,128)(2,1)S(1)}, u32[]{:S(2)}, u32[]{:S(2)}) collective-permute-start(bf16[8,8,32,384]{3,2,1,0:T(8,128)(2,1)S(1)} %get-tuple-element.21), channel_id=1, source_target_pairs={{0,1},{1,0},{2,3},{3,2},{4,5},{5,4},{6,7},{7,6},{8,9},{9,8},{10,11... | collective-permute-start | bytes 4718600 | tf_op jit(solution)/shard_map/ppermute | solution.py:254
  79.3 0.0 copy-start.1
  79.3 1.9 %copy-done.1 = bf16[4096,384]{1,0:T(8,128)(2,1)S(1)} copy-done((bf16[4096,384]{1,0:T(8,128)(2,1)S(1)}, bf16[4096,384]{1,0:T(8,128)(2,1)}, u32[]{:S(2)}) %copy-start.1) | copy-done | bytes 3145752
  81.2 2.8 %shard_map.104 = bf16[192,4096]{1,0:T(8,128)(2,1)} custom-call(bf16[192,384]{1,0:T(8,128)(2,1)S(1)} %get-tuple-element.22.grad_ref, bf16[4096,384]{1,0:T(8,128)(2,1)S(1)} %copy-done.1), custom_call_target="tpu_custom_call" | custom-call | flops 603979776 | bytes 4718592 | tf_op jit(solution)/shard_map/pallas_call | solution.py:177
  84.0 0.0 collective-permute-done.3
  84.0 0.5 add_convert_fusion
  84.5 24.9 %all_to_all.22 = bf16[8,8,32,384]{3,2,1,0:T(8,128)(2,1)S(1)} all-to-all(bf16[8,8,32,384]{3,2,1,0:T(8,128)(2,1)S(1)} %add_convert_fusion), channel_id=1, replica_groups={{0,4,32,36,128,132,160,164},{8,12,40,44,136,140,168,172},{16,20,48,52,1..., dimensions={0} | all-to-all | bytes 3145728 | tf_op jit(solution)/shard_map/all_to_all | solution.py:42
  109.4 0.2 reduce_sum.21
  109.6 0.1 reshape.23
  109.7 29.4 %all_to_all.23 = bf16[64,4,384]{2,1,0:T(4,128)(2,1)S(1)} all-to-all(bf16[64,4,384]{2,1,0:T(4,128)(2,1)S(1)} %reshape.23), channel_id=1, replica_groups=mesh['zh'=4,'zl'=2,'xlh'=2,'xll'=2,'yh'=4,'yl'=2,'xh'=2,'c'=2] {'zh','xl..., dimensions={0} | all-to-all | bytes 393216 | tf_op jit(solution)/shard_map/all_to_all | solution.py:270
  139.1 0.6 fusion.2
  (6 shorter events, 0.1 us)
Async XLA Ops:
  28.6 29.7 %copy-start.2 = (bf16[1,192,4096]{2,1,0:T(8,128)(2,1)S(1)}, bf16[1,192,4096]{2,1,0:T(8,128)(2,1)}, u32[]{:S(2)}) copy-start(bf16[1,192,4096]{2,1,0:T(8,128)(2,1)} %param.6) | copy-start | bytes 4718596
  52.9 5.4 %collective-permute-start = (bf16[8,8,32,384]{3,2,1,0:T(8,128)(2,1)S(1)}, bf16[8,8,32,384]{3,2,1,0:T(8,128)(2,1)}, u32[]{:S(2)}, u32[]{:S(2)}) collective-permute-start(bf16[8,8,32,384]{3,2,1,0:T(8,128)(2,1)S(1)} %all_to_all.21.mine_ref), channel_id=1, source_target_pairs={{0,1},{1,0},{2,3},{3,2},{4,5},{5,4},{6,7},{7,6},{8,9},{9,8},{10,11... | collective-permute-start | bytes 4718600 | tf_op jit(solution)/shard_map/ppermute | solution.py:205
  58.3 8.4 %copy-start.3 = (bf16[1,192,128]{2,1,0:T(8,128)(2,1)S(1)}, bf16[1,192,128]{2,1,0:T(8,128)(2,1)}, u32[]{:S(2)}) copy-start(bf16[1,192,128]{2,1,0:T(8,128)(2,1)} %param.11) | copy-start | bytes 147460
  61.5 1.6 %copy-start = (bf16[4096,384]{1,0:T(8,128)(2,1)}, bf16[4096,384]{1,0:T(8,128)(2,1)S(1)}, u32[]{:S(2)}) copy-start(bf16[4096,384]{1,0:T(8,128)(2,1)S(1)} %get-tuple-element.23.weight_ref) | copy-start | bytes 9437188
  63.2 3.6 %collective-permute-start.1 = (bf16[192,256]{1,0:T(8,128)(2,1)S(1)}, bf16[192,256]{1,0:T(8,128)(2,1)S(1)}, u32[]{:S(2)}, u32[]{:S(2)}) collective-permute-start(bf16[192,256]{1,0:T(8,128)(2,1)S(1)} %slice.12), channel_id=1, source_target_pairs={{0,32},{32,64},{64,96},{96,128},{128,160},{160,192},{192,224},{224... | collective-permute-start | bytes 294920 | tf_op jit(solution)/shard_map/ppermute | solution.py:47
  68.2 6.6 %collective-permute-start.2 = (bf16[192,256]{1,0:T(8,128)(2,1)S(1)}, bf16[192,256]{1,0:T(8,128)(2,1)S(1)}, u32[]{:S(2)}, u32[]{:S(2)}) collective-permute-start(bf16[192,256]{1,0:T(8,128)(2,1)S(1)} %get-tuple-element.20), channel_id=1, source_target_pairs={{32,0},{64,32},{96,64},{128,96},{160,128},{192,160},{224,192},{256... | collective-permute-start | bytes 294920 | tf_op jit(solution)/shard_map/ppermute | solution.py:47
  76.1 7.9 %collective-permute-start.3 = (bf16[8,8,32,384]{3,2,1,0:T(8,128)(2,1)S(1)}, bf16[8,8,32,384]{3,2,1,0:T(8,128)(2,1)S(1)}, u32[]{:S(2)}, u32[]{:S(2)}) collective-permute-start(bf16[8,8,32,384]{3,2,1,0:T(8,128)(2,1)S(1)} %get-tuple-element.21), channel_id=1, source_target_pairs={{0,1},{1,0},{2,3},{3,2},{4,5},{5,4},{6,7},{7,6},{8,9},{9,8},{10,11... | collective-permute-start | bytes 4718600 | tf_op jit(solution)/shard_map/ppermute | solution.py:254
  79.3 1.9 %copy-start.1 = (bf16[4096,384]{1,0:T(8,128)(2,1)S(1)}, bf16[4096,384]{1,0:T(8,128)(2,1)}, u32[]{:S(2)}) copy-start(bf16[4096,384]{1,0:T(8,128)(2,1)} %copy-done) | copy-start | bytes 9437188

commit v4 on v3

--- a/solution.py
+++ b/solution.py
@@ -76,69 +76,95 @@
 
 
 def attend_kernel(
-    qkv_ref, earlier_ref, query_ids_ref, key_ids_ref, upstream_ref, attn_ref, dq_ref, own_ref, back_ref
+    core_ref,
+    tok_ref,
+    qkv_ref,
+    earlier_ref,
+    later_ref,
+    prior_ids_ref,
+    ids_ref,
+    next_ids_ref,
+    upstream_ref,
+    attn_ref,
+    grad_ref,
+    mine_ref,
+    other_ref,
+    tok_rows,
+    tok_here,
 ):
-    tok_count, heads = dq_ref.shape
+    fetch = pltpu.make_async_copy(tok_ref, tok_rows, tok_here)
+    fetch.start()
+    tok_count, heads = attn_ref.shape
     scale = 1.0 / math.sqrt(heads)
-    query = qkv_ref[:, :heads]
-    keys = jnp.concatenate([earlier_ref[:, :heads], qkv_ref[:, heads : 2 * heads]], axis=0)
-    values = jnp.concatenate([earlier_ref[:, heads:], qkv_ref[:, 2 * heads :]], axis=0)
-    upstream = upstream_ref[...]
     across, over = (((1,), (1,)), ((), ())), (((0,), (0,)), ((), ()))
+    rows = lax.broadcasted_iota(jnp.int32, (tok_count, 2 * tok_count), 0)
+    columns = lax.broadcasted_iota(jnp.int32, (tok_count, 2 * tok_count), 1)
+    causal = columns <= rows + tok_count
+    diagonal = rows[:, :tok_count] == columns[:, :tok_count]
+    prior_ids, own_ids, next_ids = (
+        ref[...].astype(jnp.float32) for ref in (prior_ids_ref, ids_ref, next_ids_ref)
+    )
 
     def dot(a, b, dims):
         return lax.dot_general(a, b, dims, preferred_element_type=jnp.float32)
 
-    rows = lax.broadcasted_iota(jnp.int32, (tok_count, 2 * tok_count), 0)
-    columns = lax.broadcasted_iota(jnp.int32, (tok_count, 2 * tok_count), 1)
-    allowed = (columns <= rows + tok_count) & (key_ids_ref[...] == query_ids_ref[...])
-    scores = jnp.where(allowed, dot(query, keys, across) * scale, -1e30)
-    peak = jnp.max(scores, axis=-1, keepdims=True)
-    raised = jnp.where(allowed, jnp.exp(scores - peak), 0.0)
-    prob = raised / jnp.sum(raised, axis=-1, keepdims=True)
-    prob_b = prob.astype(jnp.bfloat16)
-    dprob = dot(upstream, values, across)
-    delta = jnp.sum(prob * dprob, axis=-1, keepdims=True)
-    dscore = (prob * (dprob - delta) * scale).astype(jnp.bfloat16)
-    dk = dot(dscore, query, over)
-    dv = dot(prob_b, upstream, over)
-    back_ref[:, :heads] = dk[:tok_count].astype(jnp.bfloat16)
-    back_ref[:, heads:] = dv[:tok_count].astype(jnp.bfloat16)
-    own_ref[:, :heads] = dk[tok_count:]
-    own_ref[:, heads:] = dv[tok_count:]
-    dq_ref[...] = jnp.dot(dscore, keys, preferred_element_type=jnp.float32).astype(jnp.bfloat16)
+    def attend(query, keys, values, upstream, before, ids):
+        query_ids = jnp.sum(jnp.where(diagonal, ids, 0.0), axis=1, keepdims=True)
+        allowed = causal & (jnp.concatenate([before, ids], axis=1) == query_ids)
+        scores = jnp.where(allowed, dot(query, keys, across) * scale, -1e30)
+        peak = jnp.max(scores, axis=-1, keepdims=True)
+        raised = jnp.where(allowed, jnp.exp(scores - peak), 0.0)
+        prob = raised / jnp.sum(raised, axis=-1, keepdims=True)
+        dprob = dot(upstream, values, across)
+        delta = jnp.sum(prob * dprob, axis=-1, keepdims=True)
+        dscore = (prob * (dprob - delta) * scale).astype(jnp.bfloat16)
+        return prob.astype(jnp.bfloat16), dscore
+
+    query, upstream = qkv_ref[:, :heads], upstream_ref[...]
+    own_keys, own_values = qkv_ref[:, heads : 2 * heads], qkv_ref[:, 2 * heads :]
+    keys = jnp.concatenate([earlier_ref[:, :heads], own_keys], axis=0)
+    values = jnp.concatenate([earlier_ref[:, heads:], own_values], axis=0)
+    prob_b, dscore = attend(query, keys, values, upstream, prior_ids, own_ids)
     attn_ref[...] = jnp.dot(prob_b, values, preferred_element_type=jnp.float32).astype(jnp.bfloat16)
-
-
-def term_kernel(core_ref, tok_ref, dq_ref, own_ref, back_ref, mine_ref, other_ref, grad_ref):
+    dq = jnp.dot(dscore, keys, preferred_element_type=jnp.float32)
+
+    later_query, later_upstream = later_ref[:, :heads], later_ref[:, 3 * heads :]
+    keys = jnp.concatenate([own_keys, later_ref[:, heads : 2 * heads]], axis=0)
+    values = jnp.concatenate([own_values, later_ref[:, 2 * heads : 3 * heads]], axis=0)
+    later_prob_b, later_dscore = attend(
+        later_query, keys, values, later_upstream, own_ids, next_ids
+    )
+    dk = dot(dscore, query, over)[tok_count:] + dot(later_dscore, later_query, over)[:tok_count]
+    dv = dot(prob_b, upstream, over)[tok_count:] + dot(later_prob_b, later_upstream, over)[:tok_count]
+    for i, grad in enumerate((dq, dk, dv)):
+        grad_ref[:, i * heads : (i + 1) * heads] = grad.astype(jnp.bfloat16)
+
+    fetch.wait()
     first = core_ref[0] == 0
-    heads = dq_ref.shape[1]
-    grad_ref[:, :heads] = dq_ref[...]
-    grad_ref[:, heads:] = (own_ref[...] + back_ref[...].astype(jnp.float32)).astype(jnp.bfloat16)
     grad = grad_ref[...]
-    columns = grad.shape[1]
-    low = lax.broadcasted_iota(jnp.int32, (8, 8, columns), 1) < 4
+    width = grad.shape[1]
+    low = lax.broadcasted_iota(jnp.int32, (8, 8, width), 1) < 4
     for zh in range(4):
         for zl in range(2):
             for xlh in range(2):
                 for xll in range(2):
                     f = fsdp_index(zh, zl, xlh, xll)
                     term = lax.dot_general(
-                        tok_ref[:, f * 128 : (f + 1) * 128],
+                        tok_rows[:, f * 128 : (f + 1) * 128],
                         grad,
                         (((0,), (0,)), ((), ())),
                         preferred_element_type=jnp.float32,
                     )
-                    by_hi = term.reshape(8, 2, 8, columns)
+                    by_hi = term.reshape(8, 2, 8, width)
                     even, odd = by_hi[:, 0], by_hi[:, 1]
                     zero = jnp.where(low, even, pltpu.roll(odd, 4, 1))
                     one = jnp.where(low, pltpu.roll(even, 4, 1), odd)
-                    mine = jnp.where(first, zero, one).reshape(4, 2, 8, columns)
-                    other = jnp.where(first, one, zero).reshape(4, 2, 8, columns)
+                    mine = jnp.where(first, zero, one).reshape(4, 2, 8, width)
+                    other = jnp.where(first, one, zero).reshape(4, 2, 8, width)
                     for yl in range(2):
                         at = (zl * 2 + xll) * 2 + yl, zh * 2 + xlh
-                        mine_ref[at] = mine[:, yl].reshape(32, columns).astype(jnp.bfloat16)
-                        other_ref[at] = other[:, yl].reshape(32, columns).astype(jnp.bfloat16)
+                        mine_ref[at] = mine[:, yl].reshape(32, width).astype(jnp.bfloat16)
+                        other_ref[at] = other[:, yl].reshape(32, width).astype(jnp.bfloat16)
 
 
 def back_kernel(grad_ref, weight_ref, out_ref, *scratch):
@@ -171,7 +197,7 @@
 
 def call(kernel, outs, flops, moved, *args, far_args=(), far_outs=(), scratch=()):
     def space(i, array, far):
-        return whole(pl.ANY if i in far else pltpu.SMEM if array.ndim == 1 else pltpu.VMEM)
+        return whole(pltpu.HBM if i in far else pltpu.SMEM if array.ndim == 1 else pltpu.VMEM)
 
     shapes = [jax.ShapeDtypeStruct(shape, dtype) for shape, dtype in outs]
     return pl.pallas_call(
@@ -189,7 +215,7 @@
     tok_rows = tokens[0]
     tok_count, depth = tok_rows.shape
     heads = w_query.shape[1]
-    bf16, f32 = jnp.bfloat16, jnp.float32
+    bf16 = jnp.bfloat16
     core = lax.axis_index("c")
     core_arg = core.reshape(1).astype(jnp.int32)
     flops, moved = 2 * tok_count * depth * 3 * heads, 3 * 2 * tok_count * depth
@@ -216,40 +242,37 @@
         scratch=[weight_part] * 4 + [pltpu.SemaphoreType.DMA((4,))],
     )
 
-    first_row = lax.axis_index(FSDP) * tok_count
-    id_line = segment_ids[0]
-    own_ids = lax.dynamic_slice_in_dim(id_line, first_row, tok_count)
-    prior_ids = lax.dynamic_slice_in_dim(id_line, jnp.maximum(first_row - tok_count, 0), tok_count)
-    prior_ids = jnp.where(first_row > 0, prior_ids, -1)
-    attn, query_gradient, own_parts, back_parts = call(
+    device = lax.axis_index(FSDP)
+    prior_ids, own_ids, next_ids = (
+        lax.dynamic_slice_in_dim(segment_ids, jnp.clip(device + i, 0, 31) * tok_count, tok_count, axis=1)
+        for i in (-1, 0, 1)
+    )
+    prior_ids = jnp.where(device > 0, prior_ids, -1)
+    next_ids = jnp.where(device < 31, next_ids, -2)
+    earlier = shifted(qkv_rounded[:, heads:], 1)
+    later = shifted(jnp.concatenate([qkv_rounded, grad_out[0]], axis=1), -1)
+    parts = (8, 8, 32, 3 * heads)
+    attn, grad_proj, mine, other = call(
         attend_kernel,
         [
             ((tok_count, heads), bf16),
-            ((tok_count, heads), bf16),
-            ((tok_count, 2 * heads), f32),
-            ((tok_count, 2 * heads), bf16),
+            ((tok_count, 3 * heads), bf16),
+            (parts, bf16),
+            (parts, bf16),
         ],
-        7 * 4 * tok_count * tok_count * heads,
-        12 * tok_count * heads,
-        qkv_rounded,
-        shifted(qkv_rounded[:, heads:], 1),
-        own_ids[:, None],
-        jnp.concatenate([prior_ids, own_ids])[None, :],
-        grad_out[0],
-    )
-    returned = shifted(back_parts, -1)
-
-    parts = (8, 8, 32, 3 * heads)
-    mine, other, grad_proj = call(
-        term_kernel,
-        [(parts, bf16), (parts, bf16), ((tok_count, 3 * heads), bf16)],
-        flops,
+        flops + 14 * 4 * tok_count * tok_count * heads,
         moved,
         core_arg,
-        tok_rows,
-        query_gradient,
-        own_parts,
-        returned,
+        pltpu.with_memory_space_constraint(tok_rows, pltpu.HBM),
+        qkv_rounded,
+        earlier,
+        later,
+        prior_ids,
+        own_ids,
+        next_ids,
+        grad_out[0],
+        far_args=(1,),
+        scratch=[pltpu.VMEM((tok_count, depth), bf16), pltpu.SemaphoreType.DMA],
     )
     swapped = lax.ppermute(other, "c", SWAP)
     (grad_input,) = call(

time: 140 us -> 131 us (0.936)
  waiting for transfers between devices: 10 us -> 5.85 us
  blocking collectives: 106 us -> 102 us
  local copies, waits for them, and re-layouts: 4.49 us -> 0.85 us
  starting transfers between devices: 7.66 us -> 10 us
    ppermute x2, waiting for transfers between devices: 7.35 us -> 2.24 us  [shifted(): return lax.ppermute(block, FSDP, route)]
    unnamed x8 -> x4, local copies, waits for them, and re-layouts: 3.53 us -> 0.01 us
    ppermute x2, starting transfers between devices: 2.57 us -> 5.27 us  [shifted(): return lax.ppermute(block, FSDP, route)]
    all_to_all x2, blocking collectives: 49.2 us -> 47.2 us  [cube_exchange(): return lax.all_to_all(block, FSDP + DP, 0, 0, axis_index_groups=cubes())]
    all_to_all x1, blocking collectives: 29.4 us -> 28 us  [local(): rows = lax.all_to_all(rows, ('zh', 'xlh', 'yh', 'xh'), 0, 0)]
    pallas_call x4 -> x3, Pallas kernels: 8.8 us -> 7.92 us  [call(): pl.pallas_call(kernel, out_shape=shapes, in_specs=[space(i, arg, far_args...]
  transfers between devices with their start and end apart: 4 -> 4, of which waited for: 3 -> 4; matrix products, arithmetic and copies ran while one was open for 1% -> 1% of each run, Pallas kernels for 2% -> 2%
where the time goes in v4:
time: 131 us
  blocking collectives  102 us (78%)
  starting transfers between devices  10 us (8%)
  Pallas kernels  7.92 us (6%)
  waiting for transfers between devices  5.85 us (4%)
  other arithmetic  3.04 us (2%)
    all_to_all x2, blocking collectives, cube_exchange(): return lax.all_to_all(block, FSDP + DP, 0, 0, axis_index_groups=cubes())  47.2 us
    all_to_all x1, blocking collectives, local(): rows = lax.all_to_all(rows, ('zh', 'xlh', 'yh', 'xh'), 0, 0)  28 us
    all_to_all x1, blocking collectives, local(): lax.all_to_all(jnp.broadcast_to(quarter, (8,) + quarter.shape), ('zh', 'x...  27 us
    pallas_call x3, Pallas kernels, call(): pl.pallas_call(kernel, out_shape=shapes, in_specs=[space(i, arg, far_args...  7.92 us
    ppermute x2, starting transfers between devices, shifted(): return lax.ppermute(block, FSDP, route)  5.27 us
    ppermute x1, waiting for transfers between devices, local(): other_half = lax.ppermute(half, 'c', SWAP)  3.38 us
    ppermute x1, starting transfers between devices, local(): swapped = lax.ppermute(other, 'c', SWAP)  2.87 us
  transfers between devices with their start and end apart: 4, of which 4 were waited for; matrix products, arithmetic and copies ran while one was open for 1% of the time, Pallas kernels for 2%

profile of v4, /device:TPU:1, one launch (start us, length us, event | category | flops | bytes accessed | tf_op | source)
XLA Modules:
  0.0 130.7 jit_solution(1899524293518788212)
XLA Ops:
  0.6 0.7 fusion.1
  1.4 27.0 %all_to_all.20 = bf16[8,32,384]{2,1,0:T(8,128)(2,1)S(1)} all-to-all(bf16[8,32,384]{2,1,0:T(8,128)(2,1)S(1)} %broadcast_in_dim.19), channel_id=1, replica_groups=mesh['zh'=4,'zl'=2,'xlh'=2,'xll'=2,'yh'=4,'yl'=2,'xh'=2,'c'=2] {'zh','xlh'}, dimensions={0} | all-to-all | bytes 393216 | tf_op jit(solution)/shard_map/all_to_all | solution.py:229
  28.4 0.2 broadcast_in_dim.20
  28.6 0.0 copy-start
  28.6 24.3 %all_to_all.21.mine_ref = bf16[8,8,32,384]{3,2,1,0:T(8,128)(2,1)S(1)} all-to-all(bf16[8,8,32,384]{3,2,1,0:T(8,128)(2,1)S(1)} %broadcast_in_dim.20), channel_id=1, replica_groups={{0,4,32,36,128,132,160,164},{8,12,40,44,136,140,168,172},{16,20,48,52,1..., dimensions={0} | all-to-all | bytes 3145728 | tf_op jit(solution)/shard_map/all_to_all | solution.py:42
  52.9 1.9 %collective-permute-start = (bf16[8,8,32,384]{3,2,1,0:T(8,128)(2,1)S(1)}, bf16[8,8,32,384]{3,2,1,0:T(8,128)(2,1)S(1)}, u32[]{:S(2)}, u32[]{:S(2)}) collective-permute-start(bf16[8,8,32,384]{3,2,1,0:T(8,128)(2,1)S(1)} %all_to_all.21.mine_ref), channel_id=1, source_target_pairs={{0,1},{1,0},{2,3},{3,2},{4,5},{5,4},{6,7},{7,6},{8,9},{9,8},{10,11... | collective-permute-start | bytes 4718600 | tf_op jit(solution)/shard_map/ppermute | solution.py:231
  54.8 3.4 %collective-permute-done.other_ref = bf16[8,8,32,384]{3,2,1,0:T(8,128)(2,1)S(1)} collective-permute-done((bf16[8,8,32,384]{3,2,1,0:T(8,128)(2,1)S(1)}, bf16[8,8,32,384]{3,2,1,0:T(8,128)(2,1)S(1)}, u32[]{:S(2)}, u32[]{:S(2)}) %collective-permute-start) | collective-permute-done | bytes 1572896 | tf_op jit(solution)/shard_map/ppermute | solution.py:231
  58.2 0.0 copy-done
  58.2 0.0 copy-start.1
  58.2 1.8 %shard_map.101 = (bf16[4096,384]{1,0:T(8,128)(2,1)S(1)}, bf16[192,384]{1,0:T(8,128)(2,1)S(1)}) custom-call(s32[1]{0:T(128)} %bitcast.core_ref, bf16[192,4096]{1,0:T(8,128)(2,1)S(1)} %bitcast.6, bf16[8,8,32,384]{3,2,1,0:T(8,128)(2,1)S(1)} %all_to_all.21.mine_ref, bf16[8,8,32,384]{3,2,1,0:T(8,128)(2,1)S(1)} %collective-permute-done.other_ref), custom_call_target="tpu_custom_call" | custom-call | flops 603979776 | bytes 4718592 | tf_op jit(solution)/shard_map/pallas_call | solution.py:203
  60.0 0.0 copy-done.1
  60.0 0.7 pad_maximum_fusion
  60.7 1.3 collective-permute-start.2
  62.0 4.0 %collective-permute-start.1 = (bf16[192,256]{1,0:T(8,128)(2,1)S(1)}, bf16[192,256]{1,0:T(8,128)(2,1)S(1)}, u32[]{:S(2)}, u32[]{:S(2)}) collective-permute-start(bf16[192,256]{1,0:T(8,128)(2,1)S(1)} %slice.12), channel_id=1, source_target_pairs={{0,32},{32,64},{64,96},{96,128},{128,160},{160,192},{192,224},{224... | collective-permute-start | bytes 294920 | tf_op jit(solution)/shard_map/ppermute | solution.py:47
  66.0 0.9 broadcast_select_fusion
  66.9 0.7 collective-permute-done.1.earlier_ref
  67.6 1.5 %collective-permute-done.2.later_ref = bf16[192,512]{1,0:T(8,128)(2,1)S(1)} collective-permute-done((bf16[192,512]{1,0:T(8,128)(2,1)}, bf16[192,512]{1,0:T(8,128)(2,1)S(1)}, u32[]{:S(2)}, u32[]{:S(2)}) %collective-permute-start.2) | collective-permute-done | bytes 196640 | tf_op jit(solution)/shard_map/ppermute | solution.py:47
  69.1 3.4 %shard_map.102 = (bf16[192,128]{1,0:T(8,128)(2,1)}, bf16[192,384]{1,0:T(8,128)(2,1)S(1)}, bf16[8,8,32,384]{3,2,1,0:T(8,128)(2,1)S(1)}, bf16[8,8,32,384]{3,2,1,0:T(8,128)(2,1)S(1)}) custom-call(s32[1]{0:T(128)} %bitcast.core_ref, bf16[192,4096]{1,0:T(8,128)(2,1)} %bitcast.5, bf16[192,384]{1,0:T(8,128)(2,1)S(1)} %get-tuple-element.13.qkv_ref, ...), custom_call_target="tpu_custom_call" | custom-call | flops 868220928 | bytes 4718592 | tf_op jit(solution)/shard_map/pallas_call | solution.py:203
  72.5 2.9 %collective-permute-start.3 = (bf16[8,8,32,384]{3,2,1,0:T(8,128)(2,1)S(1)}, bf16[8,8,32,384]{3,2,1,0:T(8,128)(2,1)S(1)}, u32[]{:S(2)}, u32[]{:S(2)}) collective-permute-start(bf16[8,8,32,384]{3,2,1,0:T(8,128)(2,1)S(1)} %get-tuple-element.15), channel_id=1, source_target_pairs={{0,1},{1,0},{2,3},{3,2},{4,5},{5,4},{6,7},{7,6},{8,9},{9,8},{10,11... | collective-permute-start | bytes 4718600 | tf_op jit(solution)/shard_map/ppermute | solution.py:277
  75.4 2.8 %shard_map.103 = bf16[192,4096]{1,0:T(8,128)(2,1)} custom-call(bf16[192,384]{1,0:T(8,128)(2,1)S(1)} %get-tuple-element.16.grad_ref, bf16[4096,384]{1,0:T(8,128)(2,1)S(1)} %get-tuple-element.17.weight_ref), custom_call_target="tpu_custom_call" | custom-call | flops 603979776 | bytes 4718592 | tf_op jit(solution)/shard_map/pallas_call | solution.py:203
  78.1 0.2 collective-permute-done.3
  78.4 0.4 add_convert_fusion
  78.8 23.0 %all_to_all.22 = bf16[8,8,32,384]{3,2,1,0:T(8,128)(2,1)S(1)} all-to-all(bf16[8,8,32,384]{3,2,1,0:T(8,128)(2,1)S(1)} %add_convert_fusion), channel_id=1, replica_groups={{0,4,32,36,128,132,160,164},{8,12,40,44,136,140,168,172},{16,20,48,52,1..., dimensions={0} | all-to-all | bytes 3145728 | tf_op jit(solution)/shard_map/all_to_all | solution.py:42
  101.8 0.2 reduce_sum.21
  102.0 0.1 reshape.17
  102.1 28.0 %all_to_all.23 = bf16[64,4,384]{2,1,0:T(4,128)(2,1)S(1)} all-to-all(bf16[64,4,384]{2,1,0:T(4,128)(2,1)S(1)} %reshape.17), channel_id=1, replica_groups=mesh['zh'=4,'zl'=2,'xlh'=2,'xll'=2,'yh'=4,'yl'=2,'xh'=2,'c'=2] {'zh','xl..., dimensions={0} | all-to-all | bytes 393216 | tf_op jit(solution)/shard_map/all_to_all | solution.py:293
  130.1 0.6 fusion.2
  (4 shorter events, 0.1 us)
Async XLA Ops:
  28.6 29.6 %copy-start = (bf16[1,192,4096]{2,1,0:T(8,128)(2,1)S(1)}, bf16[1,192,4096]{2,1,0:T(8,128)(2,1)}, u32[]{:S(2)}) copy-start(bf16[1,192,4096]{2,1,0:T(8,128)(2,1)} %param.6) | copy-start | bytes 4718596
  52.9 5.3 %collective-permute-start = (bf16[8,8,32,384]{3,2,1,0:T(8,128)(2,1)S(1)}, bf16[8,8,32,384]{3,2,1,0:T(8,128)(2,1)S(1)}, u32[]{:S(2)}, u32[]{:S(2)}) collective-permute-start(bf16[8,8,32,384]{3,2,1,0:T(8,128)(2,1)S(1)} %all_to_all.21.mine_ref), channel_id=1, source_target_pairs={{0,1},{1,0},{2,3},{3,2},{4,5},{5,4},{6,7},{7,6},{8,9},{9,8},{10,11... | collective-permute-start | bytes 4718600 | tf_op jit(solution)/shard_map/ppermute | solution.py:231
  58.2 1.8 %copy-start.1 = (bf16[1,192,128]{2,1,0:T(8,128)(2,1)S(1)}, bf16[1,192,128]{2,1,0:T(8,128)(2,1)}, u32[]{:S(2)}) copy-start(bf16[1,192,128]{2,1,0:T(8,128)(2,1)} %param.11) | copy-start | bytes 147460
  60.7 8.4 %collective-permute-start.2 = (bf16[192,512]{1,0:T(8,128)(2,1)}, bf16[192,512]{1,0:T(8,128)(2,1)S(1)}, u32[]{:S(2)}, u32[]{:S(2)}) collective-permute-start(bf16[192,512]{1,0:T(8,128)(2,1)} %pad_maximum_fusion), channel_id=1, source_target_pairs={{32,0},{64,32},{96,64},{128,96},{160,128},{192,160},{224,192},{256... | collective-permute-start | bytes 589832 | tf_op jit(solution)/shard_map/ppermute | solution.py:47
  62.0 5.6 %collective-permute-start.1 = (bf16[192,256]{1,0:T(8,128)(2,1)S(1)}, bf16[192,256]{1,0:T(8,128)(2,1)S(1)}, u32[]{:S(2)}, u32[]{:S(2)}) collective-permute-start(bf16[192,256]{1,0:T(8,128)(2,1)S(1)} %slice.12), channel_id=1, source_target_pairs={{0,32},{32,64},{64,96},{96,128},{128,160},{160,192},{192,224},{224... | collective-permute-start | bytes 294920 | tf_op jit(solution)/shard_map/ppermute | solution.py:47
  72.5 5.9 %collective-permute-start.3 = (bf16[8,8,32,384]{3,2,1,0:T(8,128)(2,1)S(1)}, bf16[8,8,32,384]{3,2,1,0:T(8,128)(2,1)S(1)}, u32[]{:S(2)}, u32[]{:S(2)}) collective-permute-start(bf16[8,8,32,384]{3,2,1,0:T(8,128)(2,1)S(1)} %get-tuple-element.15), channel_id=1, source_target_pairs={{0,1},{1,0},{2,3},{3,2},{4,5},{5,4},{6,7},{7,6},{8,9},{9,8},{10,11... | collective-permute-start | bytes 4718600 | tf_op jit(solution)/shard_map/ppermute | solution.py:277

commit v5 on v4

--- a/solution.py
+++ b/solution.py
@@ -47,7 +47,11 @@
     return lax.ppermute(block, FSDP, route)
 
 
-def project_kernel(core_ref, tok_ref, mine_ref, other_ref, weight_ref, qkv_ref, *scratch):
+def project_kernel(
+    core_ref, tok_ref, mine_ref, other_ref, upstream_ref, weight_ref, sent_ref, *scratch
+):
+    heads = upstream_ref.shape[1]
+    sent_ref[:, 3 * heads :] = upstream_ref[...]
     core = core_ref[0]
     total, copies = None, []
     for zh in range(4):
@@ -70,7 +74,7 @@
             tok_ref[:, zh * rows : (zh + 1) * rows], part_ref[...], preferred_element_type=jnp.float32
         )
         total = term if total is None else total + term
-    qkv_ref[...] = total.astype(jnp.bfloat16)
+    sent_ref[:, : 3 * heads] = total.astype(jnp.bfloat16)
     for copy in copies:
         copy.wait()
 
@@ -78,13 +82,12 @@
 def attend_kernel(
     core_ref,
     tok_ref,
-    qkv_ref,
+    sent_ref,
     earlier_ref,
     later_ref,
     prior_ids_ref,
     ids_ref,
     next_ids_ref,
-    upstream_ref,
     attn_ref,
     grad_ref,
     mine_ref,
@@ -120,8 +123,8 @@
         dscore = (prob * (dprob - delta) * scale).astype(jnp.bfloat16)
         return prob.astype(jnp.bfloat16), dscore
 
-    query, upstream = qkv_ref[:, :heads], upstream_ref[...]
-    own_keys, own_values = qkv_ref[:, heads : 2 * heads], qkv_ref[:, 2 * heads :]
+    query, upstream = sent_ref[:, :heads], sent_ref[:, 3 * heads :]
+    own_keys, own_values = sent_ref[:, heads : 2 * heads], sent_ref[:, 2 * heads : 3 * heads]
     keys = jnp.concatenate([earlier_ref[:, :heads], own_keys], axis=0)
     values = jnp.concatenate([earlier_ref[:, heads:], own_values], axis=0)
     prob_b, dscore = attend(query, keys, values, upstream, prior_ids, own_ids)
@@ -229,15 +232,16 @@
     far = lax.all_to_all(jnp.broadcast_to(quarter, (8,) + quarter.shape), ("zh", "xlh"), 0, 0)
     half = cube_exchange(jnp.broadcast_to(far, (8,) + far.shape))
     other_half = lax.ppermute(half, "c", SWAP)
-    full_weight, qkv_rounded = call(
+    full_weight, sent = call(
         project_kernel,
-        [((depth, 3 * heads), bf16), ((tok_count, 3 * heads), bf16)],
+        [((depth, 3 * heads), bf16), ((tok_count, 4 * heads), bf16)],
         flops,
         moved,
         core_arg,
         tok_rows,
         half,
         other_half,
+        grad_out[0],
         far_outs=(0,),
         scratch=[weight_part] * 4 + [pltpu.SemaphoreType.DMA((4,))],
     )
@@ -249,8 +253,8 @@
     )
     prior_ids = jnp.where(device > 0, prior_ids, -1)
     next_ids = jnp.where(device < 31, next_ids, -2)
-    earlier = shifted(qkv_rounded[:, heads:], 1)
-    later = shifted(jnp.concatenate([qkv_rounded, grad_out[0]], axis=1), -1)
+    earlier = shifted(sent[:, heads : 3 * heads], 1)
+    later = shifted(sent, -1)
     parts = (8, 8, 32, 3 * heads)
     attn, grad_proj, mine, other = call(
         attend_kernel,
@@ -264,13 +268,12 @@
         moved,
         core_arg,
         pltpu.with_memory_space_constraint(tok_rows, pltpu.HBM),
-        qkv_rounded,
+        sent,
         earlier,
         later,
         prior_ids,
         own_ids,
         next_ids,
-        grad_out[0],
         far_args=(1,),
         scratch=[pltpu.VMEM((tok_count, depth), bf16), pltpu.SemaphoreType.DMA],
     )

time: 131 us -> 130 us (level)
  no operation moved by 1% of the time
where the time goes in v5:
time: 130 us
  blocking collectives  102 us (78%)
  starting transfers between devices  10.1 us (8%)
  Pallas kernels  7.93 us (6%)
  waiting for transfers between devices  5.64 us (4%)
  other arithmetic  2.34 us (2%)
    all_to_all x2, blocking collectives, cube_exchange(): return lax.all_to_all(block, FSDP + DP, 0, 0, axis_index_groups=cubes())  47.3 us
    all_to_all x1, blocking collectives, local(): rows = lax.all_to_all(rows, ('zh', 'xlh', 'yh', 'xh'), 0, 0)  28.1 us
    all_to_all x1, blocking collectives, local(): lax.all_to_all(jnp.broadcast_to(quarter, (8,) + quarter.shape), ('zh', 'x...  27 us
    pallas_call x3, Pallas kernels, call(): pl.pallas_call(kernel, out_shape=shapes, in_specs=[space(i, arg, far_args...  7.93 us
    ppermute x2, starting transfers between devices, shifted(): return lax.ppermute(block, FSDP, route)  5.28 us
    ppermute x1, waiting for transfers between devices, local(): other_half = lax.ppermute(half, 'c', SWAP)  3.38 us
    ppermute x1, starting transfers between devices, local(): swapped = lax.ppermute(other, 'c', SWAP)  2.86 us
  transfers between devices with their start and end apart: 4, of which 4 were waited for; matrix products, arithmetic and copies ran while one was open for 1% of the time, Pallas kernels for 2%

profile of v5, /device:TPU:1, one launch (start us, length us, event | category | flops | bytes accessed | tf_op | source)
XLA Modules:
  0.0 130.0 jit_solution(14135960812773734929)
XLA Ops:
  0.6 0.7 fusion.1
  1.4 27.0 %all_to_all.20 = bf16[8,32,384]{2,1,0:T(8,128)(2,1)S(1)} all-to-all(bf16[8,32,384]{2,1,0:T(8,128)(2,1)S(1)} %broadcast_in_dim.19), channel_id=1, replica_groups=mesh['zh'=4,'zl'=2,'xlh'=2,'xll'=2,'yh'=4,'yl'=2,'xh'=2,'c'=2] {'zh','xlh'}, dimensions={0} | all-to-all | bytes 393216 | tf_op jit(solution)/shard_map/all_to_all | solution.py:232
  28.4 0.2 broadcast_in_dim.20
  28.6 0.0 copy-start
  28.6 0.0 copy-start.1
  28.6 24.3 %all_to_all.21.mine_ref = bf16[8,8,32,384]{3,2,1,0:T(8,128)(2,1)S(1)} all-to-all(bf16[8,8,32,384]{3,2,1,0:T(8,128)(2,1)S(1)} %broadcast_in_dim.20), channel_id=1, replica_groups={{0,4,32,36,128,132,160,164},{8,12,40,44,136,140,168,172},{16,20,48,52,1..., dimensions={0} | all-to-all | bytes 3145728 | tf_op jit(solution)/shard_map/all_to_all | solution.py:42
  52.9 1.9 %collective-permute-start = (bf16[8,8,32,384]{3,2,1,0:T(8,128)(2,1)S(1)}, bf16[8,8,32,384]{3,2,1,0:T(8,128)(2,1)S(1)}, u32[]{:S(2)}, u32[]{:S(2)}) collective-permute-start(bf16[8,8,32,384]{3,2,1,0:T(8,128)(2,1)S(1)} %all_to_all.21.mine_ref), channel_id=1, source_target_pairs={{0,1},{1,0},{2,3},{3,2},{4,5},{5,4},{6,7},{7,6},{8,9},{9,8},{10,11... | collective-permute-start | bytes 4718600 | tf_op jit(solution)/shard_map/ppermute | solution.py:234
  54.8 3.4 %collective-permute-done.other_ref = bf16[8,8,32,384]{3,2,1,0:T(8,128)(2,1)S(1)} collective-permute-done((bf16[8,8,32,384]{3,2,1,0:T(8,128)(2,1)S(1)}, bf16[8,8,32,384]{3,2,1,0:T(8,128)(2,1)S(1)}, u32[]{:S(2)}, u32[]{:S(2)}) %collective-permute-start) | collective-permute-done | bytes 1572896 | tf_op jit(solution)/shard_map/ppermute | solution.py:234
  58.2 0.0 copy-done
  58.2 0.0 copy-done.1
  58.2 1.8 %shard_map.101 = (bf16[4096,384]{1,0:T(8,128)(2,1)S(1)}, bf16[192,512]{1,0:T(8,128)(2,1)S(1)}) custom-call(s32[1]{0:T(128)} %bitcast.core_ref, bf16[192,4096]{1,0:T(8,128)(2,1)S(1)} %bitcast.6, bf16[8,8,32,384]{3,2,1,0:T(8,128)(2,1)S(1)} %all_to_all.21.mine_ref, bf16[8,8,32,384]{3,2,1,0:T(8,128)(2,1)S(1)} %collective-permute-done.other_ref, ...), custom_call_target="tpu_custom_call" | custom-call | flops 603979776 | bytes 4718592 | tf_op jit(solution)/shard_map/pallas_call | solution.py:206
  60.0 1.3 collective-permute-start.2
  61.3 4.0 %collective-permute-start.1 = (bf16[192,256]{1,0:T(8,128)(2,1)S(1)}, bf16[192,256]{1,0:T(8,128)(2,1)S(1)}, u32[]{:S(2)}, u32[]{:S(2)}) collective-permute-start(bf16[192,256]{1,0:T(8,128)(2,1)S(1)} %slice.12), channel_id=1, source_target_pairs={{0,32},{32,64},{64,96},{96,128},{128,160},{160,192},{192,224},{224... | collective-permute-start | bytes 294920 | tf_op jit(solution)/shard_map/ppermute | solution.py:47
  65.3 0.9 broadcast_select_fusion
  66.2 0.7 collective-permute-done.1.earlier_ref
  66.9 1.3 %collective-permute-done.2.later_ref = bf16[192,512]{1,0:T(8,128)(2,1)S(1)} collective-permute-done((bf16[192,512]{1,0:T(8,128)(2,1)S(1)}, bf16[192,512]{1,0:T(8,128)(2,1)S(1)}, u32[]{:S(2)}, u32[]{:S(2)}) %collective-permute-start.2) | collective-permute-done | bytes 196640 | tf_op jit(solution)/shard_map/ppermute | solution.py:47
  68.2 3.4 %shard_map.102 = (bf16[192,128]{1,0:T(8,128)(2,1)}, bf16[192,384]{1,0:T(8,128)(2,1)S(1)}, bf16[8,8,32,384]{3,2,1,0:T(8,128)(2,1)S(1)}, bf16[8,8,32,384]{3,2,1,0:T(8,128)(2,1)S(1)}) custom-call(s32[1]{0:T(128)} %bitcast.core_ref, bf16[192,4096]{1,0:T(8,128)(2,1)} %bitcast.5, bf16[192,512]{1,0:T(8,128)(2,1)S(1)} %get-tuple-element.13.sent_ref, ...), custom_call_target="tpu_custom_call" | custom-call | flops 868220928 | bytes 4718592 | tf_op jit(solution)/shard_map/pallas_call | solution.py:206
  71.6 2.9 %collective-permute-start.3 = (bf16[8,8,32,384]{3,2,1,0:T(8,128)(2,1)S(1)}, bf16[8,8,32,384]{3,2,1,0:T(8,128)(2,1)S(1)}, u32[]{:S(2)}, u32[]{:S(2)}) collective-permute-start(bf16[8,8,32,384]{3,2,1,0:T(8,128)(2,1)S(1)} %get-tuple-element.15), channel_id=1, source_target_pairs={{0,1},{1,0},{2,3},{3,2},{4,5},{5,4},{6,7},{7,6},{8,9},{9,8},{10,11... | collective-permute-start | bytes 4718600 | tf_op jit(solution)/shard_map/ppermute | solution.py:280
  74.5 2.8 %shard_map.103 = bf16[192,4096]{1,0:T(8,128)(2,1)} custom-call(bf16[192,384]{1,0:T(8,128)(2,1)S(1)} %get-tuple-element.16.grad_ref, bf16[4096,384]{1,0:T(8,128)(2,1)S(1)} %get-tuple-element.17.weight_ref), custom_call_target="tpu_custom_call" | custom-call | flops 603979776 | bytes 4718592 | tf_op jit(solution)/shard_map/pallas_call | solution.py:206
  77.3 0.2 collective-permute-done.3
  77.5 0.4 add_convert_fusion
  77.9 23.0 %all_to_all.22 = bf16[8,8,32,384]{3,2,1,0:T(8,128)(2,1)S(1)} all-to-all(bf16[8,8,32,384]{3,2,1,0:T(8,128)(2,1)S(1)} %add_convert_fusion), channel_id=1, replica_groups={{0,4,32,36,128,132,160,164},{8,12,40,44,136,140,168,172},{16,20,48,52,1..., dimensions={0} | all-to-all | bytes 3145728 | tf_op jit(solution)/shard_map/all_to_all | solution.py:42
  101.0 0.2 reduce_sum.21
  101.2 0.1 reshape.17
  101.2 28.1 %all_to_all.23 = bf16[64,4,384]{2,1,0:T(4,128)(2,1)S(1)} all-to-all(bf16[64,4,384]{2,1,0:T(4,128)(2,1)S(1)} %reshape.17), channel_id=1, replica_groups=mesh['zh'=4,'zl'=2,'xlh'=2,'xll'=2,'yh'=4,'yl'=2,'xh'=2,'c'=2] {'zh','xl..., dimensions={0} | all-to-all | bytes 393216 | tf_op jit(solution)/shard_map/all_to_all | solution.py:296
  129.4 0.6 fusion.2
  (4 shorter events, 0.1 us)
Async XLA Ops:
  28.6 29.6 %copy-start = (bf16[1,192,4096]{2,1,0:T(8,128)(2,1)S(1)}, bf16[1,192,4096]{2,1,0:T(8,128)(2,1)}, u32[]{:S(2)}) copy-start(bf16[1,192,4096]{2,1,0:T(8,128)(2,1)} %param.6) | copy-start | bytes 4718596
  28.6 29.6 %copy-start.1 = (bf16[1,192,128]{2,1,0:T(8,128)(2,1)S(1)}, bf16[1,192,128]{2,1,0:T(8,128)(2,1)}, u32[]{:S(2)}) copy-start(bf16[1,192,128]{2,1,0:T(8,128)(2,1)} %param.11) | copy-start | bytes 147460
  52.9 5.3 %collective-permute-start = (bf16[8,8,32,384]{3,2,1,0:T(8,128)(2,1)S(1)}, bf16[8,8,32,384]{3,2,1,0:T(8,128)(2,1)S(1)}, u32[]{:S(2)}, u32[]{:S(2)}) collective-permute-start(bf16[8,8,32,384]{3,2,1,0:T(8,128)(2,1)S(1)} %all_to_all.21.mine_ref), channel_id=1, source_target_pairs={{0,1},{1,0},{2,3},{3,2},{4,5},{5,4},{6,7},{7,6},{8,9},{9,8},{10,11... | collective-permute-start | bytes 4718600 | tf_op jit(solution)/shard_map/ppermute | solution.py:234
  60.0 8.3 %collective-permute-start.2 = (bf16[192,512]{1,0:T(8,128)(2,1)S(1)}, bf16[192,512]{1,0:T(8,128)(2,1)S(1)}, u32[]{:S(2)}, u32[]{:S(2)}) collective-permute-start(bf16[192,512]{1,0:T(8,128)(2,1)S(1)} %get-tuple-element.13.sent_ref), channel_id=1, source_target_pairs={{32,0},{64,32},{96,64},{128,96},{160,128},{192,160},{224,192},{256... | collective-permute-start | bytes 589832 | tf_op jit(solution)/shard_map/ppermute | solution.py:47
  61.3 5.6 %collective-permute-start.1 = (bf16[192,256]{1,0:T(8,128)(2,1)S(1)}, bf16[192,256]{1,0:T(8,128)(2,1)S(1)}, u32[]{:S(2)}, u32[]{:S(2)}) collective-permute-start(bf16[192,256]{1,0:T(8,128)(2,1)S(1)} %slice.12), channel_id=1, source_target_pairs={{0,32},{32,64},{64,96},{96,128},{128,160},{160,192},{192,224},{224... | collective-permute-start | bytes 294920 | tf_op jit(solution)/shard_map/ppermute | solution.py:47
  71.6 5.9 %collective-permute-start.3 = (bf16[8,8,32,384]{3,2,1,0:T(8,128)(2,1)S(1)}, bf16[8,8,32,384]{3,2,1,0:T(8,128)(2,1)S(1)}, u32[]{:S(2)}, u32[]{:S(2)}) collective-permute-start(bf16[8,8,32,384]{3,2,1,0:T(8,128)(2,1)S(1)} %get-tuple-element.15), channel_id=1, source_target_pairs={{0,1},{1,0},{2,3},{3,2},{4,5},{5,4},{6,7},{7,6},{8,9},{9,8},{10,11... | collective-permute-start | bytes 4718600 | tf_op jit(solution)/shard_map/ppermute | solution.py:280

commit v6 on v5

--- a/solution.py
+++ b/solution.py
@@ -45,6 +45,20 @@
 def shifted(block, distance):
     route = [(i - distance, i) for i in range(32) if 0 <= i - distance < 32]
     return lax.ppermute(block, FSDP, route)
+
+
+def spread_kernel(start_ref, query_ref, key_ref, value_ref, out_ref, held, done):
+    start = pl.multiple_of(start_ref[0], 32)
+    copies = [
+        pltpu.make_async_copy(ref.at[pl.ds(start, 32), :], held.at[i], done.at[i])
+        for i, ref in enumerate((query_ref, key_ref, value_ref))
+    ]
+    for copy in copies:
+        copy.start()
+    for i, copy in enumerate(copies):
+        copy.wait()
+        for peer in range(out_ref.shape[0]):
+            out_ref[peer, :, i * 128 : (i + 1) * 128] = held[i]
 
 
 def project_kernel(
@@ -102,7 +116,6 @@
     across, over = (((1,), (1,)), ((), ())), (((0,), (0,)), ((), ()))
     rows = lax.broadcasted_iota(jnp.int32, (tok_count, 2 * tok_count), 0)
     columns = lax.broadcasted_iota(jnp.int32, (tok_count, 2 * tok_count), 1)
-    causal = columns <= rows + tok_count
     diagonal = rows[:, :tok_count] == columns[:, :tok_count]
     prior_ids, own_ids, next_ids = (
         ref[...].astype(jnp.float32) for ref in (prior_ids_ref, ids_ref, next_ids_ref)
@@ -111,9 +124,9 @@
     def dot(a, b, dims):
         return lax.dot_general(a, b, dims, preferred_element_type=jnp.float32)
 
-    def attend(query, keys, values, upstream, before, ids):
+    def attend(query, keys, values, upstream, causal, ids, key_ids):
         query_ids = jnp.sum(jnp.where(diagonal, ids, 0.0), axis=1, keepdims=True)
-        allowed = causal & (jnp.concatenate([before, ids], axis=1) == query_ids)
+        allowed = causal & (jnp.concatenate(key_ids, axis=1) == query_ids)
         scores = jnp.where(allowed, dot(query, keys, across) * scale, -1e30)
         peak = jnp.max(scores, axis=-1, keepdims=True)
         raised = jnp.where(allowed, jnp.exp(scores - peak), 0.0)
@@ -125,20 +138,22 @@
 
     query, upstream = sent_ref[:, :heads], sent_ref[:, 3 * heads :]
     own_keys, own_values = sent_ref[:, heads : 2 * heads], sent_ref[:, 2 * heads : 3 * heads]
-    keys = jnp.concatenate([earlier_ref[:, :heads], own_keys], axis=0)
-    values = jnp.concatenate([earlier_ref[:, heads:], own_values], axis=0)
-    prob_b, dscore = attend(query, keys, values, upstream, prior_ids, own_ids)
+    keys = jnp.concatenate([own_keys, earlier_ref[:, :heads]], axis=0)
+    values = jnp.concatenate([own_values, earlier_ref[:, heads:]], axis=0)
+    causal = (columns <= rows) | (columns >= tok_count)
+    prob_b, dscore = attend(query, keys, values, upstream, causal, own_ids, [own_ids, prior_ids])
     attn_ref[...] = jnp.dot(prob_b, values, preferred_element_type=jnp.float32).astype(jnp.bfloat16)
     dq = jnp.dot(dscore, keys, preferred_element_type=jnp.float32)
 
     later_query, later_upstream = later_ref[:, :heads], later_ref[:, 3 * heads :]
     keys = jnp.concatenate([own_keys, later_ref[:, heads : 2 * heads]], axis=0)
     values = jnp.concatenate([own_values, later_ref[:, 2 * heads : 3 * heads]], axis=0)
+    causal = columns <= rows + tok_count
     later_prob_b, later_dscore = attend(
-        later_query, keys, values, later_upstream, own_ids, next_ids
-    )
-    dk = dot(dscore, query, over)[tok_count:] + dot(later_dscore, later_query, over)[:tok_count]
-    dv = dot(prob_b, upstream, over)[tok_count:] + dot(later_prob_b, later_upstream, over)[:tok_count]
+        later_query, keys, values, later_upstream, causal, next_ids, [own_ids, next_ids]
+    )
+    dk = dot(dscore[:, :tok_count], query, over) + dot(later_dscore[:, :tok_count], later_query, over)
+    dv = dot(prob_b[:, :tok_count], upstream, over) + dot(later_prob_b[:, :tok_count], later_upstream, over)
     for i, grad in enumerate((dq, dk, dv)):
         grad_ref[:, i * heads : (i + 1) * heads] = grad.astype(jnp.bfloat16)
 
@@ -226,10 +241,18 @@
     weight_part = pltpu.VMEM((depth // 4, 3 * heads), bf16)
     tok_part = pltpu.VMEM((tok_count, depth // 4), bf16)
 
-    local_weight = jnp.concatenate([w_query, w_key, w_value], axis=1)
-    start = core * 64 + lax.axis_index("yl") * 32
-    quarter = lax.dynamic_slice_in_dim(local_weight, start, 32, axis=0)
-    far = lax.all_to_all(jnp.broadcast_to(quarter, (8,) + quarter.shape), ("zh", "xlh"), 0, 0)
+    start = (core * 64 + lax.axis_index("yl") * 32).reshape(1).astype(jnp.int32)
+    (quarter,) = call(
+        spread_kernel,
+        [((8, 32, 3 * heads), bf16)],
+        0,
+        9 * 32 * 3 * heads * 2,
+        start,
+        *(pltpu.with_memory_space_constraint(w, pltpu.HBM) for w in (w_query, w_key, w_value)),
+        far_args=(1, 2, 3),
+        scratch=[pltpu.VMEM((3, 32, heads), bf16), pltpu.SemaphoreType.DMA((3,))],
+    )
+    far = lax.all_to_all(quarter, ("zh", "xlh"), 0, 0)
     half = cube_exchange(jnp.broadcast_to(far, (8,) + far.shape))
     other_half = lax.ppermute(half, "c", SWAP)
     full_weight, sent = call(

time: 130 us -> 130 us (level)
    pallas_call x3 -> x4, Pallas kernels: 7.93 us -> 8.16 us  [call(): pl.pallas_call(kernel, out_shape=shapes, in_specs=[space(i, arg, far_args...]
where the time goes in v6:
time: 130 us; the launch traced here: 129 us
  blocking collectives  102 us (78%)
  starting transfers between devices  10.1 us (8%)
  Pallas kernels  8.16 us (6%)
  waiting for transfers between devices  5.64 us (4%)
  other arithmetic  1.6 us (1%)
    all_to_all x2, blocking collectives, cube_exchange(): return lax.all_to_all(block, FSDP + DP, 0, 0, axis_index_groups=cubes())  47.3 us
    all_to_all x1, blocking collectives, local(): rows = lax.all_to_all(rows, ('zh', 'xlh', 'yh', 'xh'), 0, 0)  28.1 us
    all_to_all x1, blocking collectives, local(): far = lax.all_to_all(quarter, ('zh', 'xlh'), 0, 0)  27 us
    pallas_call x4, Pallas kernels, call(): pl.pallas_call(kernel, out_shape=shapes, in_specs=[space(i, arg, far_args...  8.16 us
    ppermute x2, starting transfers between devices, shifted(): return lax.ppermute(block, FSDP, route)  5.28 us
    ppermute x1, waiting for transfers between devices, local(): other_half = lax.ppermute(half, 'c', SWAP)  3.38 us
    ppermute x1, starting transfers between devices, local(): swapped = lax.ppermute(other, 'c', SWAP)  2.87 us
  transfers between devices with their start and end apart: 4, of which 4 were waited for; matrix products, arithmetic and copies ran while one was open for 1% of the time, Pallas kernels for 2%

profile of v6, /device:TPU:1, one launch (start us, length us, event | category | flops | bytes accessed | tf_op | source)
XLA Modules:
  0.0 129.5 jit_solution(13146175405767570946)
XLA Ops:
  0.6 0.8 shard_map.101
  1.4 27.0 %all_to_all.20 = bf16[8,32,384]{2,1,0:T(8,128)(2,1)S(1)} all-to-all(bf16[8,32,384]{2,1,0:T(8,128)(2,1)S(1)} %shard_map.101), channel_id=1, replica_groups=mesh['zh'=4,'zl'=2,'xlh'=2,'xll'=2,'yh'=4,'yl'=2,'xh'=2,'c'=2] {'zh','xlh'}, dimensions={0} | all-to-all | bytes 393216 | tf_op jit(solution)/shard_map/all_to_all | solution.py:255
  28.4 0.2 broadcast_in_dim.16
  28.6 0.0 copy-start
  28.6 0.0 copy-start.1
  28.6 24.3 %all_to_all.21.mine_ref = bf16[8,8,32,384]{3,2,1,0:T(8,128)(2,1)S(1)} all-to-all(bf16[8,8,32,384]{3,2,1,0:T(8,128)(2,1)S(1)} %broadcast_in_dim.16), channel_id=1, replica_groups={{0,4,32,36,128,132,160,164},{8,12,40,44,136,140,168,172},{16,20,48,52,1..., dimensions={0} | all-to-all | bytes 3145728 | tf_op jit(solution)/shard_map/all_to_all | solution.py:42
  52.9 1.9 %collective-permute-start = (bf16[8,8,32,384]{3,2,1,0:T(8,128)(2,1)S(1)}, bf16[8,8,32,384]{3,2,1,0:T(8,128)(2,1)S(1)}, u32[]{:S(2)}, u32[]{:S(2)}) collective-permute-start(bf16[8,8,32,384]{3,2,1,0:T(8,128)(2,1)S(1)} %all_to_all.21.mine_ref), channel_id=1, source_target_pairs={{0,1},{1,0},{2,3},{3,2},{4,5},{5,4},{6,7},{7,6},{8,9},{9,8},{10,11... | collective-permute-start | bytes 4718600 | tf_op jit(solution)/shard_map/ppermute | solution.py:257
  54.8 3.4 %collective-permute-done.other_ref = bf16[8,8,32,384]{3,2,1,0:T(8,128)(2,1)S(1)} collective-permute-done((bf16[8,8,32,384]{3,2,1,0:T(8,128)(2,1)S(1)}, bf16[8,8,32,384]{3,2,1,0:T(8,128)(2,1)S(1)}, u32[]{:S(2)}, u32[]{:S(2)}) %collective-permute-start) | collective-permute-done | bytes 1572896 | tf_op jit(solution)/shard_map/ppermute | solution.py:257
  58.2 0.0 copy-done
  58.2 0.0 copy-done.1
  58.2 1.8 %shard_map.102 = (bf16[4096,384]{1,0:T(8,128)(2,1)S(1)}, bf16[192,512]{1,0:T(8,128)(2,1)S(1)}) custom-call(s32[1]{0:T(128)} %bitcast.core_ref, bf16[192,4096]{1,0:T(8,128)(2,1)S(1)} %bitcast.7, bf16[8,8,32,384]{3,2,1,0:T(8,128)(2,1)S(1)} %all_to_all.21.mine_ref, bf16[8,8,32,384]{3,2,1,0:T(8,128)(2,1)S(1)} %collective-permute-done.other_ref, ...), custom_call_target="tpu_custom_call" | custom-call | flops 603979776 | bytes 4718592 | tf_op jit(solution)/shard_map/pallas_call | solution.py:221
  60.0 1.3 collective-permute-start.2
  61.3 4.0 %collective-permute-start.1 = (bf16[192,256]{1,0:T(8,128)(2,1)S(1)}, bf16[192,256]{1,0:T(8,128)(2,1)S(1)}, u32[]{:S(2)}, u32[]{:S(2)}) collective-permute-start(bf16[192,256]{1,0:T(8,128)(2,1)S(1)} %slice.12), channel_id=1, source_target_pairs={{0,32},{32,64},{64,96},{96,128},{128,160},{160,192},{192,224},{224... | collective-permute-start | bytes 294920 | tf_op jit(solution)/shard_map/ppermute | solution.py:47
  65.3 0.9 broadcast_select_fusion
  66.2 0.7 collective-permute-done.1.earlier_ref
  66.9 1.3 %collective-permute-done.2.later_ref = bf16[192,512]{1,0:T(8,128)(2,1)S(1)} collective-permute-done((bf16[192,512]{1,0:T(8,128)(2,1)S(1)}, bf16[192,512]{1,0:T(8,128)(2,1)S(1)}, u32[]{:S(2)}, u32[]{:S(2)}) %collective-permute-start.2) | collective-permute-done | bytes 196640 | tf_op jit(solution)/shard_map/ppermute | solution.py:47
  68.2 2.8 %shard_map.103 = (bf16[192,128]{1,0:T(8,128)(2,1)}, bf16[192,384]{1,0:T(8,128)(2,1)S(1)}, bf16[8,8,32,384]{3,2,1,0:T(8,128)(2,1)S(1)}, bf16[8,8,32,384]{3,2,1,0:T(8,128)(2,1)S(1)}) custom-call(s32[1]{0:T(128)} %bitcast.core_ref, bf16[192,4096]{1,0:T(8,128)(2,1)} %bitcast.6, bf16[192,512]{1,0:T(8,128)(2,1)S(1)} %get-tuple-element.13.sent_ref, ...), custom_call_target="tpu_custom_call" | custom-call | flops 868220928 | bytes 4718592 | tf_op jit(solution)/shard_map/pallas_call | solution.py:221
  71.1 2.9 %collective-permute-start.3 = (bf16[8,8,32,384]{3,2,1,0:T(8,128)(2,1)S(1)}, bf16[8,8,32,384]{3,2,1,0:T(8,128)(2,1)S(1)}, u32[]{:S(2)}, u32[]{:S(2)}) collective-permute-start(bf16[8,8,32,384]{3,2,1,0:T(8,128)(2,1)S(1)} %get-tuple-element.15), channel_id=1, source_target_pairs={{0,1},{1,0},{2,3},{3,2},{4,5},{5,4},{6,7},{7,6},{8,9},{9,8},{10,11... | collective-permute-start | bytes 4718600 | tf_op jit(solution)/shard_map/ppermute | solution.py:303
  74.0 2.8 %shard_map.104 = bf16[192,4096]{1,0:T(8,128)(2,1)} custom-call(bf16[192,384]{1,0:T(8,128)(2,1)S(1)} %get-tuple-element.16.grad_ref, bf16[4096,384]{1,0:T(8,128)(2,1)S(1)} %get-tuple-element.17.weight_ref), custom_call_target="tpu_custom_call" | custom-call | flops 603979776 | bytes 4718592 | tf_op jit(solution)/shard_map/pallas_call | solution.py:221
  76.7 0.2 collective-permute-done.3
  77.0 0.4 add_convert_fusion
  77.4 23.0 %all_to_all.22 = bf16[8,8,32,384]{3,2,1,0:T(8,128)(2,1)S(1)} all-to-all(bf16[8,8,32,384]{3,2,1,0:T(8,128)(2,1)S(1)} %add_convert_fusion), channel_id=1, replica_groups={{0,4,32,36,128,132,160,164},{8,12,40,44,136,140,168,172},{16,20,48,52,1..., dimensions={0} | all-to-all | bytes 3145728 | tf_op jit(solution)/shard_map/all_to_all | solution.py:42
  100.4 0.2 reduce_sum.21
  100.7 0.1 reshape.21
  100.7 28.1 %all_to_all.23 = bf16[64,4,384]{2,1,0:T(4,128)(2,1)S(1)} all-to-all(bf16[64,4,384]{2,1,0:T(4,128)(2,1)S(1)} %reshape.21), channel_id=1, replica_groups=mesh['zh'=4,'zl'=2,'xlh'=2,'xll'=2,'yh'=4,'yl'=2,'xh'=2,'c'=2] {'zh','xl..., dimensions={0} | all-to-all | bytes 393216 | tf_op jit(solution)/shard_map/all_to_all | solution.py:319
  128.9 0.6 fusion
  (3 shorter events, 0.1 us)
Async XLA Ops:
  28.6 29.6 %copy-start = (bf16[1,192,4096]{2,1,0:T(8,128)(2,1)S(1)}, bf16[1,192,4096]{2,1,0:T(8,128)(2,1)}, u32[]{:S(2)}) copy-start(bf16[1,192,4096]{2,1,0:T(8,128)(2,1)} %param.6) | copy-start | bytes 4718596
  28.6 29.6 %copy-start.1 = (bf16[1,192,128]{2,1,0:T(8,128)(2,1)S(1)}, bf16[1,192,128]{2,1,0:T(8,128)(2,1)}, u32[]{:S(2)}) copy-start(bf16[1,192,128]{2,1,0:T(8,128)(2,1)} %param.11) | copy-start | bytes 147460
  52.9 5.3 %collective-permute-start = (bf16[8,8,32,384]{3,2,1,0:T(8,128)(2,1)S(1)}, bf16[8,8,32,384]{3,2,1,0:T(8,128)(2,1)S(1)}, u32[]{:S(2)}, u32[]{:S(2)}) collective-permute-start(bf16[8,8,32,384]{3,2,1,0:T(8,128)(2,1)S(1)} %all_to_all.21.mine_ref), channel_id=1, source_target_pairs={{0,1},{1,0},{2,3},{3,2},{4,5},{5,4},{6,7},{7,6},{8,9},{9,8},{10,11... | collective-permute-start | bytes 4718600 | tf_op jit(solution)/shard_map/ppermute | solution.py:257
  60.0 8.3 %collective-permute-start.2 = (bf16[192,512]{1,0:T(8,128)(2,1)S(1)}, bf16[192,512]{1,0:T(8,128)(2,1)S(1)}, u32[]{:S(2)}, u32[]{:S(2)}) collective-permute-start(bf16[192,512]{1,0:T(8,128)(2,1)S(1)} %get-tuple-element.13.sent_ref), channel_id=1, source_target_pairs={{32,0},{64,32},{96,64},{128,96},{160,128},{192,160},{224,192},{256... | collective-permute-start | bytes 589832 | tf_op jit(solution)/shard_map/ppermute | solution.py:47
  61.3 5.6 %collective-permute-start.1 = (bf16[192,256]{1,0:T(8,128)(2,1)S(1)}, bf16[192,256]{1,0:T(8,128)(2,1)S(1)}, u32[]{:S(2)}, u32[]{:S(2)}) collective-permute-start(bf16[192,256]{1,0:T(8,128)(2,1)S(1)} %slice.12), channel_id=1, source_target_pairs={{0,32},{32,64},{64,96},{96,128},{128,160},{160,192},{192,224},{224... | collective-permute-start | bytes 294920 | tf_op jit(solution)/shard_map/ppermute | solution.py:47
  71.1 5.9 %collective-permute-start.3 = (bf16[8,8,32,384]{3,2,1,0:T(8,128)(2,1)S(1)}, bf16[8,8,32,384]{3,2,1,0:T(8,128)(2,1)S(1)}, u32[]{:S(2)}, u32[]{:S(2)}) collective-permute-start(bf16[8,8,32,384]{3,2,1,0:T(8,128)(2,1)S(1)} %get-tuple-element.15), channel_id=1, source_target_pairs={{0,1},{1,0},{2,3},{3,2},{4,5},{5,4},{6,7},{7,6},{8,9},{9,8},{10,11... | collective-permute-start | bytes 4718600 | tf_op jit(solution)/shard_map/ppermute | solution.py:303
